TPU v7x, 128 devices: a whole 4x4x4 slice. The times are simulated.
128 devices in a mesh: ctx: 64 (over z_lo, y, x, core), batch: 2 (over z_hi).
Axes of the slice: x: 4, y: 4, z: 4 (z_hi: 2, z_lo: 2; z = z_hi * 2 + z_lo), core: 2. Of those that a mesh axis runs over, the one named last changes fastest.
Arguments:
- queries: bfloat16 [32768, 128], P(('batch', 'ctx')), parts along dimension 0, may hold values from -30 to 30
- keys: bfloat16 [32768, 128], P(('batch', 'ctx')), parts along dimension 0, may hold values from -30 to 30
- values: bfloat16 [32768, 128], P(('batch', 'ctx')), parts along dimension 0, may hold values from -6 to 6
- tan_queries: bfloat16 [32768, 128], P(('batch', 'ctx')), parts along dimension 0, may hold values from -6 to 6
- tan_keys: bfloat16 [32768, 128], P(('batch', 'ctx')), parts along dimension 0, may hold values from -6 to 6
- tan_values: bfloat16 [32768, 128], P(('batch', 'ctx')), parts along dimension 0, may hold values from -6 to 6
- segment_ids: int32 [32768], P(('batch', 'ctx')), parts along dimension 0, may hold values from 0 to 2, as said below
Outputs:
- attended: float32 [32768, 128], P(('batch', 'ctx')), parts along dimension 0
- tan_attended: float32 [32768, 128], P(('batch', 'ctx')), parts along dimension 0
There are 2 independent parts, one for each index of `batch`. A program takes and returns all parts, laid end to end along the dimension named above; each array names one. Nothing has to cross between parts.
Inputs may be any that keep to these rules, and one draw needn't show every extreme that they name: `segment_ids`: never falling along the tokens: clip 0, then clip 1, then padding (2) at the end; every value occurs.
All inputs are finite; a program needn't handle non-finite values.
Results may differ from a plain program's by a relative error of at most 0.0003.
Values may be sent and summed in bfloat16 or wider, within the bound.
No kernel may reach another device: no remote copies, remote signals or barrier semaphores. Data moves between devices by JAX's collectives and lax.ppermute only.
A program may use at most 128 MiB of HBM per device.

v0:
```python
import functools

import jax
import jax.numpy as jnp
import numpy as np
from jax import lax
from jax.experimental import pallas as pl
from jax.experimental.pallas import tpu as pltpu
from jax.sharding import Mesh, PartitionSpec as P

F32, BF16, I16 = jnp.float32, jnp.bfloat16, jnp.int16
AXES = ("z", "y", "x", "core")
SIZES = (2, 4, 4, 2)
ROWS = 256
WIDTH = 128
META = 16
KV_ROWS = 2 * ROWS + META
Q_ROWS = ROWS + META
SCALE = WIDTH**-0.5
LOG2E = 1.4426950408889634
BARRED = -(2.0**100)
UNSEEN = -(2.0**120)
STATE_ROWS = 408
FULL = 32767.0
VMEM = pl.BlockSpec(memory_space=pltpu.VMEM)
WAITED = pl.CostEstimate(flops=2 * 10**9, bytes_accessed=1, transcendentals=0)
LIGHT = pl.CostEstimate(flops=1, bytes_accessed=1, transcendentals=0)
SMALL = pltpu.CompilerParams(vmem_limit_bytes=8 * 2**20)
LARGE = pltpu.CompilerParams(vmem_limit_bytes=16 * 2**20)


def times(left, right):
    return lax.dot_general(left, right, (((1,), (0,)), ((), ())), preferred_element_type=F32)


def turned(block):
    return block.astype(F32).T.astype(BF16)


def pack_kernel(*refs):
    sources, (kv_out, q_out), held, done = refs[:7], refs[7:9], refs[9:16], refs[16]
    copies = [pltpu.make_async_copy(a, b, done.at[n]) for n, (a, b) in enumerate(zip(sources, held))]
    for copy in copies:
        copy.start()
    for copy in copies:
        copy.wait()
    q, k, v, tq, tk, tv, ids = held
    kv_out[0:ROWS, 0:WIDTH] = k[...]
    kv_out[0:ROWS, WIDTH : 2 * WIDTH] = tk[...]
    kv_out[ROWS : ROWS + WIDTH, :] = turned(v[...])
    kv_out[ROWS + WIDTH : 2 * ROWS, :] = turned(tv[...])
    q_out[0:WIDTH, :] = turned(tq[...])
    q_out[WIDTH : 2 * WIDTH, :] = turned(q[...])
    clip = ids[...]
    zeros = jnp.sum((clip == 0).astype(F32), axis=1, keepdims=True)
    ones = jnp.sum((clip == 1).astype(F32), axis=1, keepdims=True)
    row = lax.broadcasted_iota(jnp.int32, (META, ROWS), 0)
    meta = jnp.where(row == 0, zeros, jnp.where(row == 1, ones, 0.0)).astype(BF16)
    kv_out[2 * ROWS :, :] = meta
    q_out[ROWS:, :] = meta


def pack(q, k, v, tq, tk, tv, ids):
    return pl.pallas_call(
        pack_kernel,
        out_shape=(
            jax.ShapeDtypeStruct((KV_ROWS, ROWS), BF16),
            jax.ShapeDtypeStruct((Q_ROWS, ROWS), BF16),
        ),
        in_specs=[pl.BlockSpec(memory_space=pl.ANY)] * 7,
        out_specs=(VMEM, VMEM),
        scratch_shapes=[pltpu.VMEM((ROWS, WIDTH), BF16)] * 6
        + [pltpu.VMEM((1, ROWS), jnp.int32), pltpu.SemaphoreType.DMA((7,))],
        compiler_params=SMALL,
        cost_estimate=LIGHT,
        name="pack",
    )(*[pltpu.with_memory_space_constraint(a, pltpu.HBM) for a in (q, k, v, tq, tk, tv, ids.reshape(1, ROWS))])


def split(wide):
    high = wide.astype(BF16)
    return high, (wide - high.astype(F32)).astype(BF16)


def fold(wide, op):
    return op(wide.reshape(wide.shape[0] // 8, 8, wide.shape[1]), axis=0)


def key_marks(meta):
    zeros, ones = meta[0:1, 0:WIDTH], meta[1:2, 0:WIDTH]
    row = lax.broadcasted_iota(jnp.int32, (ROWS, WIDTH), 0).astype(F32)
    lane = lax.broadcasted_iota(jnp.int32, (ROWS, WIDTH), 1)
    first = row < zeros
    second = (row >= zeros) & (row < zeros + ones)
    open_ = ((lane == 0) & first) | ((lane == 1) & second) | (lane > 2)
    return jnp.where(open_, 0.0, BARRED).astype(BF16)


def query_marks(meta):
    zeros, ones = meta[0:1, :], meta[1:2, :]
    row = lax.broadcasted_iota(jnp.int32, (WIDTH, ROWS), 0)
    lane = lax.broadcasted_iota(jnp.int32, (WIDTH, ROWS), 1).astype(F32)
    clip = jnp.where(lane < zeros, 0, jnp.where(lane < zeros + ones, 1, 2))
    return jnp.where(row == clip, 1.0, 0.0).astype(BF16)


def coded(value, levels):
    size = jnp.maximum(jnp.abs(value), 1e-30)
    exponent = jnp.ceil(jnp.log2(size)) + 1.0
    left = value * jnp.exp2(-exponent) * FULL
    rows = [exponent]
    for _ in range(levels):
        digit = jnp.round(left)
        rows.append(digit)
        left = (left - digit) * FULL
    return rows


def decoded(rows):
    exponent, digits = rows[0], rows[1:]
    value = digits[-1] * (1.0 / FULL)
    for digit in digits[-2::-1]:
        value = (value + digit) * (1.0 / FULL)
    return value * jnp.exp2(exponent)


def blocks_of(refs):
    return [ref.at[n] for ref in refs for n in range(ref.shape[0])]


def choose_kernel(core, *refs):
    half = (len(refs) - 1) // 2
    for side in range(2):

        @pl.when(core[0] == side)
        def _(side=side):
            for n, block in enumerate(refs[side * half : (side + 1) * half]):
                refs[-1][n] = block[0]


def choose(core, first, second):
    return pl.pallas_call(
        choose_kernel,
        out_shape=jax.ShapeDtypeStruct((len(first),) + first[0].shape[1:], first[0].dtype),
        in_specs=[pl.BlockSpec(memory_space=pltpu.SMEM)] + [VMEM] * 2 * len(first),
        out_specs=VMEM,
        compiler_params=SMALL,
        cost_estimate=LIGHT,
        name="choose",
    )(core, *first, *second)


def stack_kernel(counts, *refs):
    at = 0
    for count, group in zip(counts, refs[:-1]):
        refs[-1][at : at + count] = group[0:count]
        at += count


def stack(*groups, counts):
    return pl.pallas_call(
        functools.partial(stack_kernel, counts),
        out_shape=jax.ShapeDtypeStruct((sum(counts),) + groups[0].shape[1:], groups[0].dtype),
        in_specs=[VMEM] * len(groups),
        out_specs=VMEM,
        compiler_params=SMALL,
        cost_estimate=LIGHT,
        name="stack",
    )(*groups)


def gather_kernel(*refs):
    blocks, kv, marked = blocks_of(refs[:-2]), refs[-2], refs[-1]
    for n, block in enumerate(blocks):
        kv[n] = block[...]
        rows = slice(n * ROWS, (n + 1) * ROWS)
        marked[rows, 0:WIDTH] = block[0:ROWS, 0:WIDTH]
        marked[rows, WIDTH:] = key_marks(block[2 * ROWS :, :].astype(F32))


def gather(*groups):
    blocks = sum(group.shape[0] for group in groups)
    return pl.pallas_call(
        gather_kernel,
        out_shape=(
            jax.ShapeDtypeStruct((blocks, KV_ROWS, ROWS), BF16),
            jax.ShapeDtypeStruct((blocks * ROWS, 2 * WIDTH), BF16),
        ),
        in_specs=[VMEM] * len(groups),
        out_specs=(VMEM, VMEM),
        compiler_params=SMALL,
        cost_estimate=LIGHT,
        name="gather",
    )(*groups)


def visit(q_block, kv, marked, scores, state, span):
    blocks = len(kv)
    q_marked = jnp.concatenate(
        [q_block[WIDTH : 2 * WIDTH, :], query_marks(q_block[ROWS:, :].astype(F32))], axis=0
    )
    q_both = q_block[0:ROWS, :]
    top = None
    for j in range(0, blocks, span):
        part = slice(j * ROWS, (j + span) * ROWS)
        own = times(marked[part], q_marked)
        scores[part] = own
        own_top = fold(own, jnp.max)
        top = own_top if top is None else jnp.maximum(top, own_top)
    top = jnp.max(top, axis=0, keepdims=True)
    if state is None:
        total = jnp.zeros((8, ROWS), F32)
        tilt = jnp.zeros((8, ROWS), F32)
        plain = jnp.zeros((ROWS, ROWS), F32)
        bent = jnp.zeros((WIDTH, ROWS), F32)
    else:
        total, tilt, old_top, plain, bent = state
        top = jnp.maximum(top, old_top)
        less = jnp.exp2((old_top - top) * (SCALE * LOG2E))
        total, tilt, plain, bent = total * less, tilt * less, plain * less, bent * less
    for j in range(0, blocks, span):
        part = slice(j * ROWS, (j + span) * ROWS)
        group = kv[j : j + span]
        tan_scores = times(jnp.concatenate([b[0:ROWS, :] for b in group], axis=0), q_both)
        weights = jnp.exp2((scores[part] - top) * (SCALE * LOG2E))
        tilted = weights * tan_scores
        total += fold(weights, jnp.sum)
        tilt += fold(tilted, jnp.sum)
        values = jnp.concatenate([b[ROWS : 2 * ROWS, :] for b in group], axis=1)
        high, low = split(weights)
        plain += times(values, high) + times(values, low)
        high, low = split(tilted)
        bent += times(values[0:WIDTH], high) + times(values[0:WIDTH], low)
    return total, tilt, top, plain, bent


def load_state(ref):
    return ref[384:392, :], ref[392:400, :], ref[400:401, :], ref[0:ROWS, :], ref[ROWS:384, :]


def store_state(ref, state):
    total, tilt, top, plain, bent = state
    ref[384:392, :] = total
    ref[392:400, :] = tilt
    ref[400:408, :] = jnp.broadcast_to(top, (8, ROWS))
    ref[0:ROWS, :] = plain
    ref[ROWS:384, :] = bent


def clips_met(kv, q_block):
    count = functools.reduce(jnp.add, [block[2 * ROWS :, :].astype(F32) for block in kv])
    return jnp.max((count * q_block[ROWS:, :].astype(F32))[0:2, :])


def begin_kernel(groups, span, queries, *refs):
    kv, marked, state, scores = blocks_of(refs[:groups]), refs[-3], refs[-2], refs[-1]

    def one(i, carry):
        met = clips_met(kv, queries.at[i])

        @pl.when(met > 0)
        def _():
            store_state(state.at[i], visit(queries.at[i], kv, marked, scores, None, span))

        @pl.when(met <= 0)
        def _():
            state[i] = jnp.zeros((STATE_ROWS, ROWS), F32)
            state[i, 400:408, :] = jnp.full((8, ROWS), UNSEEN, F32)

        return carry

    lax.fori_loop(0, queries.shape[0], one, 0)


def go_on_kernel(groups, span, queries, *refs):
    kv, marked, state, out, scores = blocks_of(refs[:groups]), refs[-4], refs[-3], refs[-2], refs[-1]

    def one(i, carry):
        met = clips_met(kv, queries.at[i])

        @pl.when(met > 0)
        def _():
            store_state(out.at[i], visit(queries.at[i], kv, marked, scores, load_state(state.at[i]), span))

        @pl.when(met <= 0)
        def _():
            out[i] = state[i]

        return carry

    lax.fori_loop(0, queries.shape[0], one, 0)


def end_kernel(first, groups, span, queries, *refs):
    kv, marked, state, out, last, scores = blocks_of(refs[:groups]), refs[-5], refs[-4], refs[-3], refs[-2], refs[-1]

    def one(i, carry):
        met = clips_met(kv, queries.at[first + i])

        @pl.when(met > 0)
        def _():
            store_state(last, visit(queries.at[first + i], kv, marked, scores, load_state(state.at[first + i]), span))

        @pl.when(met <= 0)
        def _():
            last[...] = state[first + i]

        total, tilt, top, plain, bent = load_state(last)
        total = jnp.sum(total, axis=0, keepdims=True)
        tilt = jnp.sum(tilt, axis=0, keepdims=True) * SCALE
        share = 1.0 / jnp.where(total > 0, total, 1.0)
        mean_tilt = tilt * share
        mean = plain[0:WIDTH] * share
        tan_mean = (bent * SCALE + plain[WIDTH:]) * share - mean_tilt * mean
        log_top = top * (SCALE * LOG2E)
        whole_top = jnp.maximum(jnp.ceil(log_top), -32768.0)
        weight = total * jnp.exp2(jnp.maximum(log_top - whole_top, -1.0))
        stats = [whole_top] + coded(weight, 2) + coded(mean_tilt, 2)
        for at, block in ((0, mean), (WIDTH, tan_mean)):
            code = coded(jnp.max(jnp.abs(block), axis=0, keepdims=True) * 1.0001, 1)
            stats += code
            step = FULL / jnp.maximum(decoded(code), 1e-30)
            out[i, at : at + WIDTH, :] = jnp.round(block * step).astype(jnp.int32).astype(I16)
        stats += [jnp.zeros((1, ROWS), F32)] * (META - len(stats))
        out[i, ROWS:, :] = jnp.concatenate(stats, axis=0).astype(jnp.int32).astype(I16)
        return carry

    lax.fori_loop(0, out.shape[0], one, 0)


def attend(queries, gathered, state=None, which=None, expect=LIGHT):
    groups, marked = gathered[:-1], gathered[-1]
    blocks = sum(group.shape[0] for group in groups)
    keys, span = blocks * ROWS, blocks // 2
    scores = pltpu.VMEM((keys, ROWS), F32)
    out_shape = jax.ShapeDtypeStruct((queries.shape[0], STATE_ROWS, ROWS), F32)
    operands, scratch, count = [queries, *groups, marked], [scores], queries.shape[0]
    if state is None:
        kernel = functools.partial(begin_kernel, len(groups), span)
    else:
        operands.append(state)
        kernel = functools.partial(go_on_kernel, len(groups), span)
    if which is not None:
        first, count = which
        kernel = functools.partial(end_kernel, first, len(groups), span)
        out_shape = jax.ShapeDtypeStruct((count, Q_ROWS, ROWS), I16)
        scratch = [pltpu.VMEM((STATE_ROWS, ROWS), F32), scores]
    return pl.pallas_call(
        kernel,
        out_shape=out_shape,
        in_specs=[VMEM] * len(operands),
        out_specs=VMEM,
        scratch_shapes=scratch,
        compiler_params=LARGE,
        cost_estimate=expect,
        name="attend",
    )(*operands)


def combine_kernel(sides, ids_ref, *refs):
    parts, (out_ref, tan_ref) = refs[:-2], refs[-2:]
    found = []
    for part in [part.at[side] for part, side in zip(parts, sides)]:
        stats = part[ROWS:, :].astype(jnp.int32).astype(F32)
        rows = [stats[r : r + 1, :] for r in range(11)]
        found.append(
            (part, rows[0], decoded(rows[1:4]), decoded(rows[4:7]), decoded(rows[7:9]), decoded(rows[9:11]))
        )
    top = functools.reduce(jnp.maximum, [f[1] for f in found])
    weights = [f[2] * jnp.exp2(f[1] - top) for f in found]
    total = functools.reduce(jnp.add, weights)
    share = 1.0 / jnp.where(total > 0, total, 1.0)
    weights = [w * share for w in weights]
    mean_tilt = functools.reduce(jnp.add, [w * f[3] for w, f in zip(weights, found)])
    result = jnp.zeros((WIDTH, ROWS), F32)
    tan_result = jnp.zeros((WIDTH, ROWS), F32)
    for weight, (part, _, _, tilt, size, tan_size) in zip(weights, found):
        mean = part[0:WIDTH, :].astype(jnp.int32).astype(F32) * (size * (1.0 / FULL))
        tan_mean = part[WIDTH : 2 * WIDTH, :].astype(jnp.int32).astype(F32) * (tan_size * (1.0 / FULL))
        result += weight * mean
        tan_result += weight * tan_mean + (weight * (tilt - mean_tilt)) * mean
    valid = ids_ref[...] < 2
    out_ref[...] = jnp.where(valid, result, 0.0).T
    tan_ref[...] = jnp.where(valid, tan_result, 0.0).T


def combine(ids, parts, sides):
    shape = jax.ShapeDtypeStruct((ROWS, WIDTH), F32)
    return pl.pallas_call(
        functools.partial(combine_kernel, sides),
        out_shape=(shape, shape),
        in_specs=[VMEM] * (1 + len(parts)),
        out_specs=(VMEM, VMEM),
        compiler_params=SMALL,
        cost_estimate=LIGHT,
        name="combine",
    )(ids.reshape(1, ROWS), *parts)


def pairs_of(move):
    return [
        (i, int(np.ravel_multi_index(move(*np.unravel_index(i, SIZES)), SIZES))) for i in range(int(np.prod(SIZES)))
    ]


def route(first, second):
    return pairs_of(lambda z, y, x, c: (second if c else first)(z, y, x) + (c,))


SIBLING = pairs_of(lambda z, y, x, c: (z, y, x, 1 - c))
RIGHT = route(*[lambda z, y, x: (z, y, (x + 1) % 4)] * 2)
LEFT = route(*[lambda z, y, x: (z, y, (x + 3) % 4)] * 2)
BOTH_WAYS = route(lambda z, y, x: (z, y, (x + 1) % 4), lambda z, y, x: (z, y, (x + 3) % 4))
LEVEL = route(*[lambda z, y, x: (z, y ^ 1, x)] * 2)
Q_Z = route(*[lambda z, y, x: (1 - z, y, x)] * 2)
Q_Y = route(*[lambda z, y, x: (z, (y + 2) % 4, x)] * 2)
Q_FAR = route(*[lambda z, y, x: (1 - z, (y + 2) % 4, x)] * 2)


def back(pairs):
    return [(b, a) for a, b in pairs]


def together(*arrays):
    return lax.optimization_barrier(arrays)


def per_device(queries, keys, values, tan_queries, tan_keys, tan_values, segment_ids):
    move = functools.partial(lax.ppermute, axis_name=AXES)

    def sibling(group):
        return move(group, perm=SIBLING)

    def both(group):
        return [group, sibling(group)]

    core = lax.axis_index("core").reshape(1)
    kv, q = pack(queries, keys, values, tan_queries, tan_keys, tan_values, segment_ids)
    kv, q = kv[None], q[None]
    level = move(kv, perm=LEVEL)
    right, left = move(kv, perm=RIGHT), move(kv, perm=LEFT)
    q_z, q_y = move(q, perm=Q_Z), move(q, perm=Q_Y)
    level, right, left, q_z = together(level, right, left, q_z)
    level_right, level_left = move(level, perm=RIGHT), move(level, perm=LEFT)
    first = gather(*both(kv), *both(level), *both(right), *both(left))
    held = stack(q_z, q, counts=(1, 1))
    state = attend(held, first)

    level_right, level_left, q_y, state = together(level_right, level_left, q_y, state)
    on = move(choose(core, (right, level_right), (left, level_left)), perm=BOTH_WAYS)
    q_far = move(q_y, perm=Q_Z)
    more = both(level_right) + both(level_left)
    y_state = attend(q_y, first, expect=WAITED)
    *more, y_state = together(*more, y_state)
    second = gather(*more)
    state = attend(held, second, state)
    y_state = attend(q_y, second, y_state)

    on, q_far, state, y_state = together(on, q_far, state, y_state)
    on_other = sibling(on)
    far_state = attend(q_far, second, attend(q_far, first, expect=WAITED), expect=WAITED)
    on_other, far_state = together(on_other, far_state)
    third = gather(on, on_other)
    out_far, y_state = together(attend(q_far, third, far_state, (0, 1)), y_state)
    out_y, state = together(attend(q_y, third, y_state, (0, 1)), state)
    out_z, state = together(attend(held, third, state, (0, 1)), state)
    back_z = move(out_z, perm=back(Q_Z))
    back_y = move(out_y, perm=back(Q_Y))
    back_far = move(out_far, perm=back(Q_FAR))
    back_far, state = together(back_far, state)
    mine = attend(held, third, state, (1, 1))
    return combine(segment_ids, together(mine, back_z, back_y, back_far), (0, 0, 0, 0))


def solution(mesh):
    fine = Mesh(mesh.devices.reshape(SIZES + (2,)), AXES + ("batch",))
    rows = P(("batch",) + AXES)
    table = P(("batch",) + AXES, None)
    return jax.shard_map(
        per_device,
        mesh=fine,
        in_specs=(table,) * 6 + (rows,),
        out_specs=(table, table),
        check_vma=False,
    )
```

profile of v0, /device:TPU:64, one launch (start us, length us, event | category | flops | bytes accessed | tf_op | source)
XLA Modules:
  0.0 58.4 jit_solution(16008679244122098578)
XLA Ops:
  0.6 1.3 %pack.1 = (bf16[528,256]{1,0:T(8,128)(2,1)S(1)}, bf16[272,256]{1,0:T(8,128)(2,1)S(1)}) custom-call(bf16[256,128]{1,0:T(8,128)(2,1)} %refs_0_.1, bf16[256,128]{1,0:T(8,128)(2,1)} %refs_1_.1, bf16[256,128]{1,0:T(8,128)(2,1)} %refs_2_.1, bf16[256,128]{1,0:T(8,128)(2,1)} %refs_3_.1, bf16[256,128]{1,0:T(8,128)(2,1)} %refs_4_.1, bf16[256,128]{1,0:T(8,128)(2,1)} %refs_5_.1, ...), custom_call_target="tpu_custom_call" | custom-call | flops 1 | bytes 1 | tf_op jit(solution)/shard_map/pack/pallas_call | solution.py:64
  1.9 2.8 %collective-permute-start.2 = (bf16[1,528,256]{2,1,0:T(8,128)(2,1)S(1)}, bf16[1,528,256]{2,1,0:T(8,128)(2,1)S(1)}, u32[]{:S(2)}, u32[]{:S(2)}) collective-permute-start(bf16[1,528,256]{2,1,0:T(8,128)(2,1)S(1)} %bitcast.4), channel_id=1, source_target_pairs={{0,12},{2,14},{4,0},{6,2},{8,4},{10,6},{12,8},{14,10},{16,28},{18,... | collective-permute-start | bytes 811016 | tf_op jit(solution)/shard_map/ppermute | solution.py:441
  4.7 0.0 collective-permute-start.1
  4.7 1.6 %collective-permute-start = (bf16[1,528,256]{2,1,0:T(8,128)(2,1)S(1)}, bf16[1,528,256]{2,1,0:T(8,128)(2,1)S(1)}, u32[]{:S(2)}, u32[]{:S(2)}) collective-permute-start(bf16[1,528,256]{2,1,0:T(8,128)(2,1)S(1)} %bitcast.6), channel_id=1, source_target_pairs={{0,16},{2,18},{4,20},{6,22},{8,24},{10,26},{12,28},{14,30},{16,0},... | collective-permute-start | bytes 811016 | tf_op jit(solution)/shard_map/ppermute | solution.py:440
  6.3 1.6 %collective-permute-start.3 = (bf16[1,272,256]{2,1,0:T(8,128)(2,1)S(1)}, bf16[1,272,256]{2,1,0:T(8,128)(2,1)S(1)}, u32[]{:S(2)}, u32[]{:S(2)}) collective-permute-start(bf16[1,272,256]{2,1,0:T(8,128)(2,1)S(1)} %bitcast.9), channel_id=1, source_target_pairs={{0,64},{2,66},{4,68},{6,70},{8,72},{10,74},{12,76},{14,78},{16,80}... | collective-permute-start | bytes 417800 | tf_op jit(solution)/shard_map/ppermute | solution.py:442
  7.9 0.0 collective-permute-start.7
  7.9 3.4 %collective-permute-done.3.refs_0_ = bf16[1,272,256]{2,1,0:T(8,128)(2,1)S(1)} collective-permute-done((bf16[1,272,256]{2,1,0:T(8,128)(2,1)S(1)}, bf16[1,272,256]{2,1,0:T(8,128)(2,1)S(1)}, u32[]{:S(2)}, u32[]{:S(2)}) %collective-permute-start.3) | collective-permute-done | bytes 139296 | tf_op jit(solution)/shard_map/ppermute | solution.py:442
  11.4 0.0 collective-permute-done.2.refs_6_.refs_2_
  11.4 2.5 %collective-permute-done.1.refs_4_.refs_0_ = bf16[1,528,256]{2,1,0:T(8,128)(2,1)S(1)} collective-permute-done((bf16[1,528,256]{2,1,0:T(8,128)(2,1)S(1)}, bf16[1,528,256]{2,1,0:T(8,128)(2,1)S(1)}, u32[]{:S(2)}, u32[]{:S(2)}) %collective-permute-start.1) | collective-permute-done | bytes 270368 | tf_op jit(solution)/shard_map/ppermute | solution.py:441
  13.9 0.0 collective-permute-done.refs_2_
  13.9 0.0 collective-permute-start.9
  13.9 0.5 collective-permute-start.10
  14.4 0.0 collective-permute-start.8
  14.4 1.7 %collective-permute-start.5 = (bf16[1,528,256]{2,1,0:T(8,128)(2,1)S(1)}, bf16[1,528,256]{2,1,0:T(8,128)(2,1)S(1)}, u32[]{:S(2)}, u32[]{:S(2)}) collective-permute-start(bf16[1,528,256]{2,1,0:T(8,128)(2,1)S(1)} %collective-permute-done.refs_2_), channel_id=1, source_target_pairs={{0,12},{2,14},{4,0},{6,2},{8,4},{10,6},{12,8},{14,10},{16,28},{18,... | collective-permute-start | bytes 811016 | tf_op jit(solution)/shard_map/ppermute | solution.py:444
  16.1 0.0 collective-permute-done.7.refs_1_
  16.1 0.3 collective-permute-start.4
  16.4 0.0 collective-permute-done.9.refs_5_
  16.4 3.2 %collective-permute-start.6 = (bf16[1,272,256]{2,1,0:T(8,128)(2,1)S(1)}, bf16[1,272,256]{2,1,0:T(8,128)(2,1)S(1)}, u32[]{:S(2)}, u32[]{:S(2)}) collective-permute-start(bf16[1,272,256]{2,1,0:T(8,128)(2,1)S(1)} %bitcast.10), channel_id=1, source_target_pairs={{0,32},{2,34},{4,36},{6,38},{8,40},{10,42},{12,44},{14,46},{16,48}... | collective-permute-start | bytes 417800 | tf_op jit(solution)/shard_map/ppermute | solution.py:442
  19.6 0.0 collective-permute-done.10.refs_7_
  19.7 0.0 collective-permute-done.8.refs_3_
  19.7 0.7 %gather.3 = (bf16[8,528,256]{2,1,0:T(8,128)(2,1)S(1)}, bf16[2048,256]{1,0:T(8,128)(2,1)S(1)}) custom-call(bf16[1,528,256]{2,1,0:T(8,128)(2,1)S(1)} %bitcast.8, bf16[1,528,256]{2,1,0:T(8,128)(2,1)S(1)} %collective-permute-done.7.refs_1_, bf16[1,528,256]{2,1,0:T(8,128)(2,1)S(1)} %collective-permute-done.refs_2_, ...), custom_call_target="tpu_custom_call" | custom-call | flops 1 | bytes 1 | tf_op jit(solution)/shard_map/gather/pallas_call | solution.py:183
  20.4 4.9 %attend.10.refs_2_ = f32[2,408,256]{2,1,0:T(8,128)S(1)} custom-call(bf16[2,272,256]{2,1,0:T(8,128)(2,1)S(1)} %stack.1.queries, bf16[8,528,256]{2,1,0:T(8,128)(2,1)S(1)} %get-tuple-element.47.refs_0_, bf16[2048,256]{1,0:T(8,128)(2,1)S(1)} %get-tuple-element.48.refs_1_), custom_call_target="tpu_custom_call" | custom-call | flops 1 | bytes 1 | tf_op jit(solution)/shard_map/attend/pallas_call | solution.py:348
  25.3 0.0 collective-permute-done.6.queries
  25.3 0.0 collective-permute-done.5.refs_3_.refs_2_
  25.3 0.6 %collective-permute-done.4.refs_1_.refs_0_ = bf16[1,528,256]{2,1,0:T(8,128)(2,1)S(1)} collective-permute-done((bf16[1,528,256]{2,1,0:T(8,128)(2,1)S(1)}, bf16[1,528,256]{2,1,0:T(8,128)(2,1)S(1)}, u32[]{:S(2)}, u32[]{:S(2)}) %collective-permute-start.4) | collective-permute-done | bytes 270368 | tf_op jit(solution)/shard_map/ppermute | solution.py:444
  26.0 0.1 collective-permute-start.11
  26.1 0.1 collective-permute-start.13
  26.2 0.5 collective-permute-start.14
  26.7 2.8 %collective-permute-start.12 = (bf16[1,272,256]{2,1,0:T(8,128)(2,1)S(1)}, bf16[1,272,256]{2,1,0:T(8,128)(2,1)S(1)}, u32[]{:S(2)}, u32[]{:S(2)}) collective-permute-start(bf16[1,272,256]{2,1,0:T(8,128)(2,1)S(1)} %collective-permute-done.6.queries), channel_id=1, source_target_pairs={{0,64},{2,66},{4,68},{6,70},{8,72},{10,74},{12,76},{14,78},{16,80}... | collective-permute-start | bytes 417800 | tf_op jit(solution)/shard_map/ppermute | solution.py:451
  29.4 2.4 %attend.11.refs_2_ = f32[1,408,256]{2,1,0:T(8,128)S(1)} custom-call(bf16[1,272,256]{2,1,0:T(8,128)(2,1)S(1)} %collective-permute-done.6.queries, bf16[8,528,256]{2,1,0:T(8,128)(2,1)S(1)} %get-tuple-element.47.refs_0_, bf16[2048,256]{1,0:T(8,128)(2,1)S(1)} %get-tuple-element.48.refs_1_), custom_call_target="tpu_custom_call" | custom-call | flops 2000000000 | bytes 1 | tf_op jit(solution)/shard_map/attend/pallas_call | solution.py:348
  31.9 0.0 collective-permute-done.13.refs_1_
  31.9 0.0 collective-permute-done.14.refs_3_
  31.9 0.4 gather.4
  32.3 1.6 %attend.13.refs_2_ = f32[1,408,256]{2,1,0:T(8,128)S(1)} custom-call(bf16[1,272,256]{2,1,0:T(8,128)(2,1)S(1)} %collective-permute-done.6.queries, bf16[4,528,256]{2,1,0:T(8,128)(2,1)S(1)} %get-tuple-element.56.refs_0_, bf16[1024,256]{1,0:T(8,128)(2,1)S(1)} %get-tuple-element.57.refs_1_, f32[1,408,256]{2,1,0:T(8,128)S(1)} %attend.11.refs_2_), custom_call_target="tpu_custom_call" | custom-call | flops 1 | bytes 1 | tf_op jit(solution)/shard_map/attend/pallas_call | solution.py:348
  33.9 2.8 %attend.12.refs_2_ = f32[2,408,256]{2,1,0:T(8,128)S(1)} custom-call(bf16[2,272,256]{2,1,0:T(8,128)(2,1)S(1)} %stack.1.queries, bf16[4,528,256]{2,1,0:T(8,128)(2,1)S(1)} %get-tuple-element.56.refs_0_, bf16[1024,256]{1,0:T(8,128)(2,1)S(1)} %get-tuple-element.57.refs_1_, f32[2,408,256]{2,1,0:T(8,128)S(1)} %attend.10.refs_2_), custom_call_target="tpu_custom_call" | custom-call | flops 1 | bytes 1 | tf_op jit(solution)/shard_map/attend/pallas_call | solution.py:348
  36.7 0.0 collective-permute-done.12.queries
  36.8 0.0 collective-permute-done.11.refs_0_
  36.8 0.3 collective-permute-start.15
  37.1 0.2 attend.14.refs_2_
  37.2 0.2 attend.15.refs_2_
  37.4 1.4 %collective-permute-done.15.refs_1_ = bf16[2,528,256]{2,1,0:T(8,128)(2,1)S(1)} collective-permute-done((bf16[2,528,256]{2,1,0:T(8,128)(2,1)S(1)}, bf16[2,528,256]{2,1,0:T(8,128)(2,1)S(1)}, u32[]{:S(2)}, u32[]{:S(2)}) %collective-permute-start.15) | collective-permute-done | bytes 540704 | tf_op jit(solution)/shard_map/ppermute | solution.py:432
  38.8 0.4 gather.5
  39.2 0.3 attend.16
  39.4 1.5 %attend.17 = s16[1,272,256]{2,1,0:T(8,128)(2,1)S(1)} custom-call(bf16[1,272,256]{2,1,0:T(8,128)(2,1)S(1)} %collective-permute-done.6.queries, bf16[4,528,256]{2,1,0:T(8,128)(2,1)S(1)} %get-tuple-element.63.refs_0_, bf16[1024,256]{1,0:T(8,128)(2,1)S(1)} %get-tuple-element.64.refs_1_, f32[1,408,256]{2,1,0:T(8,128)S(1)} %attend.13.refs_2_), custom_call_target="tpu_custom_call" | custom-call | flops 1 | bytes 1 | tf_op jit(solution)/shard_map/attend/pallas_call | solution.py:348
  41.0 2.9 %collective-permute-start.16 = (s16[1,272,256]{2,1,0:T(8,128)(2,1)S(1)}, s16[1,272,256]{2,1,0:T(8,128)(2,1)S(1)}, u32[]{:S(2)}, u32[]{:S(2)}) collective-permute-start(s16[1,272,256]{2,1,0:T(8,128)(2,1)S(1)} %attend.16), channel_id=1, source_target_pairs={{96,0},{98,2},{100,4},{102,6},{104,8},{106,10},{108,12},{110,14},{... | collective-permute-start | bytes 417800 | tf_op jit(solution)/shard_map/ppermute | solution.py:469
  43.9 1.5 %attend.18 = s16[1,272,256]{2,1,0:T(8,128)(2,1)S(1)} custom-call(bf16[2,272,256]{2,1,0:T(8,128)(2,1)S(1)} %stack.1.queries, bf16[4,528,256]{2,1,0:T(8,128)(2,1)S(1)} %get-tuple-element.63.refs_0_, bf16[1024,256]{1,0:T(8,128)(2,1)S(1)} %get-tuple-element.64.refs_1_, f32[2,408,256]{2,1,0:T(8,128)S(1)} %attend.12.refs_2_), custom_call_target="tpu_custom_call" | custom-call | flops 1 | bytes 1 | tf_op jit(solution)/shard_map/attend/pallas_call | solution.py:348
  45.4 0.0 copy-start
  45.4 5.0 %collective-permute-start.17 = (s16[1,272,256]{2,1,0:T(8,128)(2,1)S(1)}, s16[1,272,256]{2,1,0:T(8,128)(2,1)S(1)}, u32[]{:S(2)}, u32[]{:S(2)}) collective-permute-start(s16[1,272,256]{2,1,0:T(8,128)(2,1)S(1)} %attend.18), channel_id=1, source_target_pairs={{64,0},{66,2},{68,4},{70,6},{72,8},{74,10},{76,12},{78,14},{80,16}... | collective-permute-start | bytes 417800 | tf_op jit(solution)/shard_map/ppermute | solution.py:467
  50.4 0.0 collective-permute-start.18
  50.4 0.0 collective-permute-done.16.refs_3_
  50.4 1.5 %attend.19.refs_0_ = s16[1,272,256]{2,1,0:T(8,128)(2,1)S(1)} custom-call(bf16[2,272,256]{2,1,0:T(8,128)(2,1)S(1)} %stack.1.queries, bf16[4,528,256]{2,1,0:T(8,128)(2,1)S(1)} %get-tuple-element.63.refs_0_, bf16[1024,256]{1,0:T(8,128)(2,1)S(1)} %get-tuple-element.64.refs_1_, f32[2,408,256]{2,1,0:T(8,128)S(1)} %attend.12.refs_2_), custom_call_target="tpu_custom_call" | custom-call | flops 1 | bytes 1 | tf_op jit(solution)/shard_map/attend/pallas_call | solution.py:348
  51.9 2.5 %collective-permute-done.17.refs_1_ = s16[1,272,256]{2,1,0:T(8,128)(2,1)S(1)} collective-permute-done((s16[1,272,256]{2,1,0:T(8,128)(2,1)S(1)}, s16[1,272,256]{2,1,0:T(8,128)(2,1)S(1)}, u32[]{:S(2)}, u32[]{:S(2)}) %collective-permute-start.17) | collective-permute-done | bytes 139296 | tf_op jit(solution)/shard_map/ppermute | solution.py:467
  54.4 3.0 %collective-permute-done.18.refs_2_ = s16[1,272,256]{2,1,0:T(8,128)(2,1)S(1)} collective-permute-done((s16[1,272,256]{2,1,0:T(8,128)(2,1)S(1)}, s16[1,272,256]{2,1,0:T(8,128)(2,1)S(1)}, u32[]{:S(2)}, u32[]{:S(2)}) %collective-permute-start.18) | collective-permute-done | bytes 139296 | tf_op jit(solution)/shard_map/ppermute | solution.py:468
  57.4 0.0 copy-done
  57.4 1.0 %combine.1 = (f32[256,128]{1,0:T(8,128)}, f32[256,128]{1,0:T(8,128)}) custom-call(s32[1,256]{1,0:T(1,128)S(1)} %bitcast.13, s16[1,272,256]{2,1,0:T(8,128)(2,1)S(1)} %attend.19.refs_0_, s16[1,272,256]{2,1,0:T(8,128)(2,1)S(1)} %collective-permute-done.17.refs_1_, s16[1,272,256]{2,1,0:T(8,128)(2,1)S(1)} %collective-permute-done.18.refs_2_, ...), custom_call_target="tpu_custom_call" | custom-call | flops 1 | bytes 1 | tf_op jit(solution)/shard_map/combine/pallas_call | solution.py:389
  (2 shorter events, 0.1 us)
Async XLA Ops:
  1.9 9.5 %collective-permute-start.2 = (bf16[1,528,256]{2,1,0:T(8,128)(2,1)S(1)}, bf16[1,528,256]{2,1,0:T(8,128)(2,1)S(1)}, u32[]{:S(2)}, u32[]{:S(2)}) collective-permute-start(bf16[1,528,256]{2,1,0:T(8,128)(2,1)S(1)} %bitcast.4), channel_id=1, source_target_pairs={{0,12},{2,14},{4,0},{6,2},{8,4},{10,6},{12,8},{14,10},{16,28},{18,... | collective-permute-start | bytes 811016 | tf_op jit(solution)/shard_map/ppermute | solution.py:441
  4.7 9.2 %collective-permute-start.1 = (bf16[1,528,256]{2,1,0:T(8,128)(2,1)S(1)}, bf16[1,528,256]{2,1,0:T(8,128)(2,1)S(1)}, u32[]{:S(2)}, u32[]{:S(2)}) collective-permute-start(bf16[1,528,256]{2,1,0:T(8,128)(2,1)S(1)} %bitcast.5), channel_id=1, source_target_pairs={{0,4},{2,6},{4,8},{6,10},{8,12},{10,14},{12,0},{14,2},{16,20},{18,... | collective-permute-start | bytes 811016 | tf_op jit(solution)/shard_map/ppermute | solution.py:441
  4.7 9.2 %collective-permute-start = (bf16[1,528,256]{2,1,0:T(8,128)(2,1)S(1)}, bf16[1,528,256]{2,1,0:T(8,128)(2,1)S(1)}, u32[]{:S(2)}, u32[]{:S(2)}) collective-permute-start(bf16[1,528,256]{2,1,0:T(8,128)(2,1)S(1)} %bitcast.6), channel_id=1, source_target_pairs={{0,16},{2,18},{4,20},{6,22},{8,24},{10,26},{12,28},{14,30},{16,0},... | collective-permute-start | bytes 811016 | tf_op jit(solution)/shard_map/ppermute | solution.py:440
  6.3 5.1 %collective-permute-start.3 = (bf16[1,272,256]{2,1,0:T(8,128)(2,1)S(1)}, bf16[1,272,256]{2,1,0:T(8,128)(2,1)S(1)}, u32[]{:S(2)}, u32[]{:S(2)}) collective-permute-start(bf16[1,272,256]{2,1,0:T(8,128)(2,1)S(1)} %bitcast.9), channel_id=1, source_target_pairs={{0,64},{2,66},{4,68},{6,70},{8,72},{10,74},{12,76},{14,78},{16,80}... | collective-permute-start | bytes 417800 | tf_op jit(solution)/shard_map/ppermute | solution.py:442
  7.9 8.2 %collective-permute-start.7 = (bf16[1,528,256]{2,1,0:T(8,128)(2,1)S(1)}, bf16[1,528,256]{2,1,0:T(8,128)(2,1)S(1)}, u32[]{:S(2)}, u32[]{:S(2)}) collective-permute-start(bf16[1,528,256]{2,1,0:T(8,128)(2,1)S(1)} %bitcast.7), channel_id=1, source_target_pairs={{0,2},{2,0},{4,6},{6,4},{8,10},{10,8},{12,14},{14,12},{16,18},{18,... | collective-permute-start | bytes 811016 | tf_op jit(solution)/shard_map/ppermute | solution.py:432
  13.9 2.5 %collective-permute-start.9 = (bf16[1,528,256]{2,1,0:T(8,128)(2,1)S(1)}, bf16[1,528,256]{2,1,0:T(8,128)(2,1)S(1)}, u32[]{:S(2)}, u32[]{:S(2)}) collective-permute-start(bf16[1,528,256]{2,1,0:T(8,128)(2,1)S(1)} %collective-permute-done.1.refs_4_.refs_0_), channel_id=1, source_target_pairs={{0,2},{2,0},{4,6},{6,4},{8,10},{10,8},{12,14},{14,12},{16,18},{18,... | collective-permute-start | bytes 811016 | tf_op jit(solution)/shard_map/ppermute | solution.py:432
  13.9 5.8 %collective-permute-start.10 = (bf16[1,528,256]{2,1,0:T(8,128)(2,1)S(1)}, bf16[1,528,256]{2,1,0:T(8,128)(2,1)S(1)}, u32[]{:S(2)}, u32[]{:S(2)}) collective-permute-start(bf16[1,528,256]{2,1,0:T(8,128)(2,1)S(1)} %collective-permute-done.2.refs_6_.refs_2_), channel_id=1, source_target_pairs={{0,2},{2,0},{4,6},{6,4},{8,10},{10,8},{12,14},{14,12},{16,18},{18,... | collective-permute-start | bytes 811016 | tf_op jit(solution)/shard_map/ppermute | solution.py:432
  14.4 5.3 %collective-permute-start.8 = (bf16[1,528,256]{2,1,0:T(8,128)(2,1)S(1)}, bf16[1,528,256]{2,1,0:T(8,128)(2,1)S(1)}, u32[]{:S(2)}, u32[]{:S(2)}) collective-permute-start(bf16[1,528,256]{2,1,0:T(8,128)(2,1)S(1)} %collective-permute-done.refs_2_), channel_id=1, source_target_pairs={{0,2},{2,0},{4,6},{6,4},{8,10},{10,8},{12,14},{14,12},{16,18},{18,... | collective-permute-start | bytes 811016 | tf_op jit(solution)/shard_map/ppermute | solution.py:432
  14.4 10.9 %collective-permute-start.5 = (bf16[1,528,256]{2,1,0:T(8,128)(2,1)S(1)}, bf16[1,528,256]{2,1,0:T(8,128)(2,1)S(1)}, u32[]{:S(2)}, u32[]{:S(2)}) collective-permute-start(bf16[1,528,256]{2,1,0:T(8,128)(2,1)S(1)} %collective-permute-done.refs_2_), channel_id=1, source_target_pairs={{0,12},{2,14},{4,0},{6,2},{8,4},{10,6},{12,8},{14,10},{16,28},{18,... | collective-permute-start | bytes 811016 | tf_op jit(solution)/shard_map/ppermute | solution.py:444
  16.1 9.8 %collective-permute-start.4 = (bf16[1,528,256]{2,1,0:T(8,128)(2,1)S(1)}, bf16[1,528,256]{2,1,0:T(8,128)(2,1)S(1)}, u32[]{:S(2)}, u32[]{:S(2)}) collective-permute-start(bf16[1,528,256]{2,1,0:T(8,128)(2,1)S(1)} %collective-permute-done.refs_2_), channel_id=1, source_target_pairs={{0,4},{2,6},{4,8},{6,10},{8,12},{10,14},{12,0},{14,2},{16,20},{18,... | collective-permute-start | bytes 811016 | tf_op jit(solution)/shard_map/ppermute | solution.py:444
  16.4 8.9 %collective-permute-start.6 = (bf16[1,272,256]{2,1,0:T(8,128)(2,1)S(1)}, bf16[1,272,256]{2,1,0:T(8,128)(2,1)S(1)}, u32[]{:S(2)}, u32[]{:S(2)}) collective-permute-start(bf16[1,272,256]{2,1,0:T(8,128)(2,1)S(1)} %bitcast.10), channel_id=1, source_target_pairs={{0,32},{2,34},{4,36},{6,38},{8,40},{10,42},{12,44},{14,46},{16,48}... | collective-permute-start | bytes 417800 | tf_op jit(solution)/shard_map/ppermute | solution.py:442
  26.0 10.7 %collective-permute-start.11 = (bf16[2,528,256]{2,1,0:T(8,128)(2,1)S(1)}, bf16[2,528,256]{2,1,0:T(8,128)(2,1)S(1)}, u32[]{:S(2)}, u32[]{:S(2)}) collective-permute-start(bf16[2,528,256]{2,1,0:T(8,128)(2,1)S(1)} %choose.1), channel_id=1, source_target_pairs={{0,4},{2,14},{4,8},{6,2},{8,12},{10,6},{12,0},{14,10},{16,20},{18,... | collective-permute-start | bytes 1622024 | tf_op jit(solution)/shard_map/ppermute | solution.py:450
  26.1 5.8 %collective-permute-start.13 = (bf16[1,528,256]{2,1,0:T(8,128)(2,1)S(1)}, bf16[1,528,256]{2,1,0:T(8,128)(2,1)S(1)}, u32[]{:S(2)}, u32[]{:S(2)}) collective-permute-start(bf16[1,528,256]{2,1,0:T(8,128)(2,1)S(1)} %collective-permute-done.4.refs_1_.refs_0_), channel_id=1, source_target_pairs={{0,2},{2,0},{4,6},{6,4},{8,10},{10,8},{12,14},{14,12},{16,18},{18,... | collective-permute-start | bytes 811016 | tf_op jit(solution)/shard_map/ppermute | solution.py:432
  26.2 5.7 %collective-permute-start.14 = (bf16[1,528,256]{2,1,0:T(8,128)(2,1)S(1)}, bf16[1,528,256]{2,1,0:T(8,128)(2,1)S(1)}, u32[]{:S(2)}, u32[]{:S(2)}) collective-permute-start(bf16[1,528,256]{2,1,0:T(8,128)(2,1)S(1)} %collective-permute-done.5.refs_3_.refs_2_), channel_id=1, source_target_pairs={{0,2},{2,0},{4,6},{6,4},{8,10},{10,8},{12,14},{14,12},{16,18},{18,... | collective-permute-start | bytes 811016 | tf_op jit(solution)/shard_map/ppermute | solution.py:432
  26.7 10.1 %collective-permute-start.12 = (bf16[1,272,256]{2,1,0:T(8,128)(2,1)S(1)}, bf16[1,272,256]{2,1,0:T(8,128)(2,1)S(1)}, u32[]{:S(2)}, u32[]{:S(2)}) collective-permute-start(bf16[1,272,256]{2,1,0:T(8,128)(2,1)S(1)} %collective-permute-done.6.queries), channel_id=1, source_target_pairs={{0,64},{2,66},{4,68},{6,70},{8,72},{10,74},{12,76},{14,78},{16,80}... | collective-permute-start | bytes 417800 | tf_op jit(solution)/shard_map/ppermute | solution.py:451
  36.8 2.0 %collective-permute-start.15 = (bf16[2,528,256]{2,1,0:T(8,128)(2,1)S(1)}, bf16[2,528,256]{2,1,0:T(8,128)(2,1)S(1)}, u32[]{:S(2)}, u32[]{:S(2)}) collective-permute-start(bf16[2,528,256]{2,1,0:T(8,128)(2,1)S(1)} %collective-permute-done.11.refs_0_), channel_id=1, source_target_pairs={{0,2},{2,0},{4,6},{6,4},{8,10},{10,8},{12,14},{14,12},{16,18},{18,... | collective-permute-start | bytes 1622024 | tf_op jit(solution)/shard_map/ppermute | solution.py:432
  41.0 9.4 %collective-permute-start.16 = (s16[1,272,256]{2,1,0:T(8,128)(2,1)S(1)}, s16[1,272,256]{2,1,0:T(8,128)(2,1)S(1)}, u32[]{:S(2)}, u32[]{:S(2)}) collective-permute-start(s16[1,272,256]{2,1,0:T(8,128)(2,1)S(1)} %attend.16), channel_id=1, source_target_pairs={{96,0},{98,2},{100,4},{102,6},{104,8},{106,10},{108,12},{110,14},{... | collective-permute-start | bytes 417800 | tf_op jit(solution)/shard_map/ppermute | solution.py:469
  45.4 12.0 %copy-start = (s32[256]{0:T(256)S(1)}, s32[256]{0:T(256)}, u32[]{:S(2)}) copy-start(s32[256]{0:T(256)} %param.13) | copy-start | bytes 3076
  45.4 9.0 %collective-permute-start.17 = (s16[1,272,256]{2,1,0:T(8,128)(2,1)S(1)}, s16[1,272,256]{2,1,0:T(8,128)(2,1)S(1)}, u32[]{:S(2)}, u32[]{:S(2)}) collective-permute-start(s16[1,272,256]{2,1,0:T(8,128)(2,1)S(1)} %attend.18), channel_id=1, source_target_pairs={{64,0},{66,2},{68,4},{70,6},{72,8},{74,10},{76,12},{78,14},{80,16}... | collective-permute-start | bytes 417800 | tf_op jit(solution)/shard_map/ppermute | solution.py:467
  50.4 7.0 %collective-permute-start.18 = (s16[1,272,256]{2,1,0:T(8,128)(2,1)S(1)}, s16[1,272,256]{2,1,0:T(8,128)(2,1)S(1)}, u32[]{:S(2)}, u32[]{:S(2)}) collective-permute-start(s16[1,272,256]{2,1,0:T(8,128)(2,1)S(1)} %attend.17), channel_id=1, source_target_pairs={{32,0},{34,2},{36,4},{38,6},{40,8},{42,10},{44,12},{46,14},{48,16}... | collective-permute-start | bytes 417800 | tf_op jit(solution)/shard_map/ppermute | solution.py:468
where the time goes:
time: 58.6 us; the launch traced here: 58.4 us
  starting transfers between devices  23.3 us (40%)
  Pallas kernels  20.7 us (35%)
  waiting for transfers between devices  13.5 us (23%)
  between operations  0.85 us (1%)
    pallas_call x10, Pallas kernels, attend(): pl.pallas_call(kernel, out_shape=out_shape, in_specs=[VMEM] * len(operand...  16.9 us
    ppermute x1, starting transfers between devices, per_device(): back_z = move(out_z, perm=back(Q_Z))  4.96 us
    ppermute x2, starting transfers between devices, per_device(): q_z, q_y = (move(q, perm=Q_Z), move(q, perm=Q_Y))  4.82 us
    ppermute x2, waiting for transfers between devices, per_device(): q_z, q_y = (move(q, perm=Q_Z), move(q, perm=Q_Y))  3.43 us
    ppermute x1, waiting for transfers between devices, per_device(): back_y = move(out_y, perm=back(Q_Y))  2.96 us
    ppermute x1, starting transfers between devices, per_device(): back_far = move(out_far, perm=back(Q_FAR))  2.87 us
    ppermute x2, starting transfers between devices, per_device(): right, left = (move(kv, perm=RIGHT), move(kv, perm=LEFT))  2.83 us
    ppermute x1, starting transfers between devices, per_device(): q_far = move(q_y, perm=Q_Z)  2.76 us
  transfers between devices with their start and end apart: 19, of which 6 were waited for; matrix products, arithmetic and copies ran while one was open for 0% of the time, Pallas kernels for 28%

commit v1 on v0

--- a/solution.py
+++ b/solution.py
@@ -20,7 +20,7 @@
 LOG2E = 1.4426950408889634
 BARRED = -(2.0**100)
 UNSEEN = -(2.0**120)
-STATE_ROWS = 408
+STATE_ROWS = 424
 FULL = 32767.0
 VMEM = pl.BlockSpec(memory_space=pltpu.VMEM)
 WAITED = pl.CostEstimate(flops=2 * 10**9, bytes_accessed=1, transcendentals=0)
@@ -209,42 +209,39 @@
         top = own_top if top is None else jnp.maximum(top, own_top)
     top = jnp.max(top, axis=0, keepdims=True)
     if state is None:
-        total = jnp.zeros((8, ROWS), F32)
-        tilt = jnp.zeros((8, ROWS), F32)
-        plain = jnp.zeros((ROWS, ROWS), F32)
-        bent = jnp.zeros((WIDTH, ROWS), F32)
+        plain = jnp.zeros((ROWS + META, ROWS), F32)
+        bent = jnp.zeros((WIDTH + META, ROWS), F32)
     else:
-        total, tilt, old_top, plain, bent = state
+        old_top, plain, bent = state
         top = jnp.maximum(top, old_top)
         less = jnp.exp2((old_top - top) * (SCALE * LOG2E))
-        total, tilt, plain, bent = total * less, tilt * less, plain * less, bent * less
+        plain, bent = plain * less, bent * less
+    ones = jnp.ones((META, span * ROWS), BF16)
     for j in range(0, blocks, span):
         part = slice(j * ROWS, (j + span) * ROWS)
         group = kv[j : j + span]
         tan_scores = times(jnp.concatenate([b[0:ROWS, :] for b in group], axis=0), q_both)
         weights = jnp.exp2((scores[part] - top) * (SCALE * LOG2E))
         tilted = weights * tan_scores
-        total += fold(weights, jnp.sum)
-        tilt += fold(tilted, jnp.sum)
         values = jnp.concatenate([b[ROWS : 2 * ROWS, :] for b in group], axis=1)
+        both = jnp.concatenate([values, ones], axis=0)
+        one = jnp.concatenate([values[0:WIDTH], ones], axis=0)
         high, low = split(weights)
-        plain += times(values, high) + times(values, low)
+        plain += times(both, high) + times(both, low)
         high, low = split(tilted)
-        bent += times(values[0:WIDTH], high) + times(values[0:WIDTH], low)
-    return total, tilt, top, plain, bent
+        bent += times(one, high) + times(one, low)
+    return top, plain, bent
 
 
 def load_state(ref):
-    return ref[384:392, :], ref[392:400, :], ref[400:401, :], ref[0:ROWS, :], ref[ROWS:384, :]
+    return ref[416:417, :], ref[0:272, :], ref[272:416, :]
 
 
 def store_state(ref, state):
-    total, tilt, top, plain, bent = state
-    ref[384:392, :] = total
-    ref[392:400, :] = tilt
-    ref[400:408, :] = jnp.broadcast_to(top, (8, ROWS))
-    ref[0:ROWS, :] = plain
-    ref[ROWS:384, :] = bent
+    top, plain, bent = state
+    ref[0:272, :] = plain
+    ref[272:416, :] = bent
+    ref[416:424, :] = jnp.broadcast_to(top, (8, ROWS))
 
 
 def clips_met(kv, q_block):
@@ -265,7 +262,7 @@
         @pl.when(met <= 0)
         def _():
             state[i] = jnp.zeros((STATE_ROWS, ROWS), F32)
-            state[i, 400:408, :] = jnp.full((8, ROWS), UNSEEN, F32)
+            state[i, 416:424, :] = jnp.full((8, ROWS), UNSEEN, F32)
 
         return carry
 
@@ -291,8 +288,9 @@
     lax.fori_loop(0, queries.shape[0], one, 0)
 
 
-def end_kernel(first, groups, span, queries, *refs):
-    kv, marked, state, out, last, scores = blocks_of(refs[:groups]), refs[-5], refs[-4], refs[-3], refs[-2], refs[-1]
+def end_kernel(first, count, groups, span, queries, *refs):
+    kv, marked, state = blocks_of(refs[:groups]), refs[groups], refs[groups + 1]
+    outs, (out, last, scores) = refs[groups + 2 : -3], refs[-3:]
 
     def one(i, carry):
         met = clips_met(kv, queries.at[first + i])
@@ -305,13 +303,13 @@
         def _():
             last[...] = state[first + i]
 
-        total, tilt, top, plain, bent = load_state(last)
-        total = jnp.sum(total, axis=0, keepdims=True)
-        tilt = jnp.sum(tilt, axis=0, keepdims=True) * SCALE
+        top, plain, bent = load_state(last)
+        total = plain[ROWS : ROWS + 1]
+        tilt = bent[WIDTH : WIDTH + 1] * SCALE
         share = 1.0 / jnp.where(total > 0, total, 1.0)
         mean_tilt = tilt * share
         mean = plain[0:WIDTH] * share
-        tan_mean = (bent * SCALE + plain[WIDTH:]) * share - mean_tilt * mean
+        tan_mean = (bent[0:WIDTH] * SCALE + plain[WIDTH:ROWS]) * share - mean_tilt * mean
         log_top = top * (SCALE * LOG2E)
         whole_top = jnp.maximum(jnp.ceil(log_top), -32768.0)
         weight = total * jnp.exp2(jnp.maximum(log_top - whole_top, -1.0))
@@ -325,7 +323,9 @@
         out[i, ROWS:, :] = jnp.concatenate(stats, axis=0).astype(jnp.int32).astype(I16)
         return carry
 
-    lax.fori_loop(0, out.shape[0], one, 0)
+    lax.fori_loop(0, count, one, 0)
+    for n in range(count):
+        outs[n][0] = out[n]
 
 
 def attend(queries, gathered, state=None, which=None, expect=LIGHT):
@@ -342,19 +342,20 @@
         kernel = functools.partial(go_on_kernel, len(groups), span)
     if which is not None:
         first, count = which
-        kernel = functools.partial(end_kernel, first, len(groups), span)
-        out_shape = jax.ShapeDtypeStruct((count, Q_ROWS, ROWS), I16)
-        scratch = [pltpu.VMEM((STATE_ROWS, ROWS), F32), scores]
-    return pl.pallas_call(
+        kernel = functools.partial(end_kernel, first, count, len(groups), span)
+        out_shape = [jax.ShapeDtypeStruct((1, Q_ROWS, ROWS), I16)] * count
+        scratch = [pltpu.VMEM((count, Q_ROWS, ROWS), I16), pltpu.VMEM((STATE_ROWS, ROWS), F32), scores]
+    result = pl.pallas_call(
         kernel,
         out_shape=out_shape,
         in_specs=[VMEM] * len(operands),
-        out_specs=VMEM,
+        out_specs=VMEM if which is None else [VMEM] * count,
         scratch_shapes=scratch,
         compiler_params=LARGE,
         cost_estimate=expect,
         name="attend",
     )(*operands)
+    return result[0] if count == 1 and which is not None else result
 
 
 def combine_kernel(sides, ids_ref, *refs):
@@ -411,10 +412,10 @@
 RIGHT = route(*[lambda z, y, x: (z, y, (x + 1) % 4)] * 2)
 LEFT = route(*[lambda z, y, x: (z, y, (x + 3) % 4)] * 2)
 BOTH_WAYS = route(lambda z, y, x: (z, y, (x + 1) % 4), lambda z, y, x: (z, y, (x + 3) % 4))
-LEVEL = route(*[lambda z, y, x: (z, y ^ 1, x)] * 2)
-Q_Z = route(*[lambda z, y, x: (1 - z, y, x)] * 2)
-Q_Y = route(*[lambda z, y, x: (z, (y + 2) % 4, x)] * 2)
-Q_FAR = route(*[lambda z, y, x: (1 - z, (y + 2) % 4, x)] * 2)
+LEVEL = route(*[lambda z, y, x: (1 - z, y, x)] * 2)
+Q_NEXT = route(*[lambda z, y, x: (z, (y + 1) % 4, x)] * 2)
+Q_LAST = route(*[lambda z, y, x: (z, (y + 3) % 4, x)] * 2)
+Q_FAR = route(*[lambda z, y, x: (z, (y + 2) % 4, x)] * 2)
 
 
 def back(pairs):
@@ -439,37 +440,36 @@
     kv, q = kv[None], q[None]
     level = move(kv, perm=LEVEL)
     right, left = move(kv, perm=RIGHT), move(kv, perm=LEFT)
-    q_z, q_y = move(q, perm=Q_Z), move(q, perm=Q_Y)
-    level, right, left, q_z = together(level, right, left, q_z)
+    q_next, q_last = move(q, perm=Q_NEXT), move(q, perm=Q_LAST)
+    q_last, q_next, left, right, level = together(q_last, q_next, left, right, level)
+    q_far = move(q, perm=Q_FAR)
     level_right, level_left = move(level, perm=RIGHT), move(level, perm=LEFT)
     first = gather(*both(kv), *both(level), *both(right), *both(left))
-    held = stack(q_z, q, counts=(1, 1))
-    state = attend(held, first)
-
-    level_right, level_left, q_y, state = together(level_right, level_left, q_y, state)
+    near_held = stack(q_last, q_next, counts=(1, 1))
+    near_state = attend(near_held, first)
+
+    level_right, level_left, q_far, near_state = together(level_right, level_left, q_far, near_state)
     on = move(choose(core, (right, level_right), (left, level_left)), perm=BOTH_WAYS)
-    q_far = move(q_y, perm=Q_Z)
     more = both(level_right) + both(level_left)
-    y_state = attend(q_y, first, expect=WAITED)
-    *more, y_state = together(*more, y_state)
+    held = stack(q_far, q, counts=(1, 1))
+    state = attend(held, first, expect=WAITED)
+    *more, state = together(*more, state)
     second = gather(*more)
-    state = attend(held, second, state)
-    y_state = attend(q_y, second, y_state)
-
-    on, q_far, state, y_state = together(on, q_far, state, y_state)
+    near_state = attend(near_held, second, near_state)
+
+    on, near_state, state = together(on, near_state, state)
     on_other = sibling(on)
-    far_state = attend(q_far, second, attend(q_far, first, expect=WAITED), expect=WAITED)
-    on_other, far_state = together(on_other, far_state)
+    state = attend(held, second, state, expect=WAITED)
+    on_other, state = together(on_other, state)
     third = gather(on, on_other)
-    out_far, y_state = together(attend(q_far, third, far_state, (0, 1)), y_state)
-    out_y, state = together(attend(q_y, third, y_state, (0, 1)), state)
-    out_z, state = together(attend(held, third, state, (0, 1)), state)
-    back_z = move(out_z, perm=back(Q_Z))
-    back_y = move(out_y, perm=back(Q_Y))
+    out_far, near_state = together(attend(held, third, state, (0, 1)), near_state)
     back_far = move(out_far, perm=back(Q_FAR))
-    back_far, state = together(back_far, state)
+    out_last, out_next = attend(near_held, third, near_state, (0, 2))
+    back_next = move(out_next, perm=back(Q_NEXT))
+    back_last = move(out_last, perm=back(Q_LAST))
+    out_next, back_far, state = together(out_next, back_far, state)
     mine = attend(held, third, state, (1, 1))
-    return combine(segment_ids, together(mine, back_z, back_y, back_far), (0, 0, 0, 0))
+    return combine(segment_ids, together(mine, back_next, back_last, back_far), (0, 0, 0, 0))
 
 
 def solution(mesh):

time: 58.6 us -> 54.7 us (0.933)
  waiting for transfers between devices: 13.5 us -> 8.88 us
  Pallas kernels: 20.7 us -> 23.3 us
  starting transfers between devices: 23.3 us -> 21.3 us
    ppermute x5, waiting for transfers between devices: 8.91 us -> 5.38 us  [the longest x2 3.39 us: per_device(): q_next, q_last = (move(q, perm=Q_NEXT), move(q, perm=Q_LAST))]
    ppermute x5, starting transfers between devices: 12.5 us -> 9.79 us  [the longest x1 3.25 us: per_device(): q_far = move(q, perm=Q_FAR)]
    pallas_call x10 -> x7, Pallas kernels: 16.9 us -> 19.5 us  [attend(): pl.pallas_call(kernel, out_shape=out_shape, in_specs=[VMEM] * len(operand...]
    ppermute x2, waiting for transfers between devices: 2.52 us -> 0.01 us  [per_device(): right, left = (move(kv, perm=RIGHT), move(kv, perm=LEFT))]
    ppermute x1, waiting for transfers between devices: 0.01 us -> 2.05 us  [per_device(): move(choose(core, (right, level_right), (left, level_left)), perm=BOTH_WAYS)]
    ppermute x7, waiting for transfers between devices: 1.38 us -> 0.02 us  [sibling(): return move(group, perm=SIBLING)]
    ppermute x2, waiting for transfers between devices: 0.63 us -> 1.42 us  [per_device(): level_right, level_left = (move(level, perm=RIGHT), move(level, perm=LEFT))]
  transfers between devices with their start and end apart: 19 -> 19, of which waited for: 6 -> 5; matrix products, arithmetic and copies ran while one was open for 0% -> 0% of each run, Pallas kernels for 28% -> 35%
where the time goes in v1:
time: 54.7 us; the launch traced here: 54.3 us
  Pallas kernels  23.3 us (43%)
  starting transfers between devices  21.3 us (39%)
  waiting for transfers between devices  8.88 us (16%)
  between operations  0.82 us (1%)
    pallas_call x7, Pallas kernels, attend(): pl.pallas_call(kernel, out_shape=out_shape, in_specs=[VMEM] * len(operand...  19.5 us
    ppermute x2, waiting for transfers between devices, per_device(): q_next, q_last = (move(q, perm=Q_NEXT), move(q, perm=Q_LAST))  3.39 us
    ppermute x1, starting transfers between devices, per_device(): q_far = move(q, perm=Q_FAR)  3.25 us
    ppermute x2, starting transfers between devices, per_device(): q_next, q_last = (move(q, perm=Q_NEXT), move(q, perm=Q_LAST))  3.24 us
    ppermute x2, starting transfers between devices, per_device(): right, left = (move(kv, perm=RIGHT), move(kv, perm=LEFT))  3.24 us
    ppermute x1, starting transfers between devices, per_device(): back_far = move(out_far, perm=back(Q_FAR))  2.57 us
    ppermute x1, starting transfers between devices, per_device(): back_next = move(out_next, perm=back(Q_NEXT))  2.56 us
    ppermute x1, waiting for transfers between devices, per_device(): move(choose(core, (right, level_right), (left, level_left)), perm=BOTH_WAYS)  2.05 us
  transfers between devices with their start and end apart: 19, of which 5 were waited for; matrix products, arithmetic and copies ran while one was open for 0% of the time, Pallas kernels for 35%

profile of v1, /device:TPU:64, one launch (start us, length us, event | category | flops | bytes accessed | tf_op | source)
XLA Modules:
  0.0 54.3 jit_solution(17229218188473832661)
XLA Ops:
  0.6 1.3 %pack.1 = (bf16[528,256]{1,0:T(8,128)(2,1)S(1)}, bf16[272,256]{1,0:T(8,128)(2,1)S(1)}) custom-call(bf16[256,128]{1,0:T(8,128)(2,1)} %refs_0_.1, bf16[256,128]{1,0:T(8,128)(2,1)} %refs_1_.1, bf16[256,128]{1,0:T(8,128)(2,1)} %refs_2_.1, bf16[256,128]{1,0:T(8,128)(2,1)} %refs_3_.1, bf16[256,128]{1,0:T(8,128)(2,1)} %refs_4_.1, bf16[256,128]{1,0:T(8,128)(2,1)} %refs_5_.1, ...), custom_call_target="tpu_custom_call" | custom-call | flops 1 | bytes 1 | tf_op jit(solution)/shard_map/pack/pallas_call | solution.py:64
  1.9 1.7 %collective-permute-start.4 = (bf16[1,528,256]{2,1,0:T(8,128)(2,1)S(1)}, bf16[1,528,256]{2,1,0:T(8,128)(2,1)S(1)}, u32[]{:S(2)}, u32[]{:S(2)}) collective-permute-start(bf16[1,528,256]{2,1,0:T(8,128)(2,1)S(1)} %bitcast.4), channel_id=1, source_target_pairs={{0,64},{2,66},{4,68},{6,70},{8,72},{10,74},{12,76},{14,78},{16,80}... | collective-permute-start | bytes 811016 | tf_op jit(solution)/shard_map/ppermute | solution.py:441
  3.6 1.5 %collective-permute-start.3 = (bf16[1,528,256]{2,1,0:T(8,128)(2,1)S(1)}, bf16[1,528,256]{2,1,0:T(8,128)(2,1)S(1)}, u32[]{:S(2)}, u32[]{:S(2)}) collective-permute-start(bf16[1,528,256]{2,1,0:T(8,128)(2,1)S(1)} %bitcast.5), channel_id=1, source_target_pairs={{0,4},{2,6},{4,8},{6,10},{8,12},{10,14},{12,0},{14,2},{16,20},{18,... | collective-permute-start | bytes 811016 | tf_op jit(solution)/shard_map/ppermute | solution.py:442
  5.1 1.7 %collective-permute-start.2 = (bf16[1,528,256]{2,1,0:T(8,128)(2,1)S(1)}, bf16[1,528,256]{2,1,0:T(8,128)(2,1)S(1)}, u32[]{:S(2)}, u32[]{:S(2)}) collective-permute-start(bf16[1,528,256]{2,1,0:T(8,128)(2,1)S(1)} %bitcast.6), channel_id=1, source_target_pairs={{0,12},{2,14},{4,0},{6,2},{8,4},{10,6},{12,8},{14,10},{16,28},{18,... | collective-permute-start | bytes 811016 | tf_op jit(solution)/shard_map/ppermute | solution.py:442
  6.8 1.6 %collective-permute-start.1 = (bf16[1,272,256]{2,1,0:T(8,128)(2,1)S(1)}, bf16[1,272,256]{2,1,0:T(8,128)(2,1)S(1)}, u32[]{:S(2)}, u32[]{:S(2)}) collective-permute-start(bf16[1,272,256]{2,1,0:T(8,128)(2,1)S(1)} %bitcast.9), channel_id=1, source_target_pairs={{0,16},{2,18},{4,20},{6,22},{8,24},{10,26},{12,28},{14,30},{16,32}... | collective-permute-start | bytes 417800 | tf_op jit(solution)/shard_map/ppermute | solution.py:443
  8.4 1.7 %collective-permute-start = (bf16[1,272,256]{2,1,0:T(8,128)(2,1)S(1)}, bf16[1,272,256]{2,1,0:T(8,128)(2,1)S(1)}, u32[]{:S(2)}, u32[]{:S(2)}) collective-permute-start(bf16[1,272,256]{2,1,0:T(8,128)(2,1)S(1)} %bitcast.10), channel_id=1, source_target_pairs={{0,48},{2,50},{4,52},{6,54},{8,56},{10,58},{12,60},{14,62},{16,0},... | collective-permute-start | bytes 417800 | tf_op jit(solution)/shard_map/ppermute | solution.py:443
  10.1 3.0 %collective-permute-done.1.refs_1_ = bf16[1,272,256]{2,1,0:T(8,128)(2,1)S(1)} collective-permute-done((bf16[1,272,256]{2,1,0:T(8,128)(2,1)S(1)}, bf16[1,272,256]{2,1,0:T(8,128)(2,1)S(1)}, u32[]{:S(2)}, u32[]{:S(2)}) %collective-permute-start.1) | collective-permute-done | bytes 139296 | tf_op jit(solution)/shard_map/ppermute | solution.py:443
  13.1 0.0 collective-permute-start.8
  13.1 0.4 collective-permute-done.refs_0_
  13.5 0.0 collective-permute-done.4.refs_2_
  13.5 0.0 collective-permute-done.3.refs_4_.refs_0_
  13.5 0.0 collective-permute-done.2.refs_6_.refs_2_
  13.5 0.2 collective-permute-start.10
  13.7 0.4 collective-permute-start.11
  14.1 0.2 collective-permute-start.9
  14.2 2.0 %collective-permute-start.6 = (bf16[1,528,256]{2,1,0:T(8,128)(2,1)S(1)}, bf16[1,528,256]{2,1,0:T(8,128)(2,1)S(1)}, u32[]{:S(2)}, u32[]{:S(2)}) collective-permute-start(bf16[1,528,256]{2,1,0:T(8,128)(2,1)S(1)} %collective-permute-done.4.refs_2_), channel_id=1, source_target_pairs={{0,12},{2,14},{4,0},{6,2},{8,4},{10,6},{12,8},{14,10},{16,28},{18,... | collective-permute-start | bytes 811016 | tf_op jit(solution)/shard_map/ppermute | solution.py:446
  16.2 0.0 collective-permute-done.8.refs_1_
  16.2 0.0 collective-permute-start.5
  16.3 0.0 collective-permute-done.10.refs_5_
  16.3 3.2 %collective-permute-start.7 = (bf16[1,272,256]{2,1,0:T(8,128)(2,1)S(1)}, bf16[1,272,256]{2,1,0:T(8,128)(2,1)S(1)}, u32[]{:S(2)}, u32[]{:S(2)}) collective-permute-start(bf16[1,272,256]{2,1,0:T(8,128)(2,1)S(1)} %bitcast.11), channel_id=1, source_target_pairs={{0,32},{2,34},{4,36},{6,38},{8,40},{10,42},{12,44},{14,46},{16,48}... | collective-permute-start | bytes 417800 | tf_op jit(solution)/shard_map/ppermute | solution.py:445
  19.5 0.0 collective-permute-done.11.refs_7_
  19.5 0.0 collective-permute-done.9.refs_3_
  19.6 0.7 %gather.3 = (bf16[8,528,256]{2,1,0:T(8,128)(2,1)S(1)}, bf16[2048,256]{1,0:T(8,128)(2,1)S(1)}) custom-call(bf16[1,528,256]{2,1,0:T(8,128)(2,1)S(1)} %bitcast.8, bf16[1,528,256]{2,1,0:T(8,128)(2,1)S(1)} %collective-permute-done.8.refs_1_, bf16[1,528,256]{2,1,0:T(8,128)(2,1)S(1)} %collective-permute-done.4.refs_2_, ...), custom_call_target="tpu_custom_call" | custom-call | flops 1 | bytes 1 | tf_op jit(solution)/shard_map/gather/pallas_call | solution.py:183
  20.3 4.3 %attend.7.refs_2_ = f32[2,424,256]{2,1,0:T(8,128)S(1)} custom-call(bf16[2,272,256]{2,1,0:T(8,128)(2,1)S(1)} %stack.2.queries, bf16[8,528,256]{2,1,0:T(8,128)(2,1)S(1)} %get-tuple-element.46.refs_0_, bf16[2048,256]{1,0:T(8,128)(2,1)S(1)} %get-tuple-element.47.refs_1_), custom_call_target="tpu_custom_call" | custom-call | flops 1 | bytes 1 | tf_op jit(solution)/shard_map/attend/pallas_call | solution.py:348
  24.6 0.0 collective-permute-done.7.refs_0_
  24.6 0.0 collective-permute-done.6.refs_3_.refs_2_
  24.6 1.4 %collective-permute-done.5.refs_1_.refs_0_ = bf16[1,528,256]{2,1,0:T(8,128)(2,1)S(1)} collective-permute-done((bf16[1,528,256]{2,1,0:T(8,128)(2,1)S(1)}, bf16[1,528,256]{2,1,0:T(8,128)(2,1)S(1)}, u32[]{:S(2)}, u32[]{:S(2)}) %collective-permute-start.5) | collective-permute-done | bytes 270368 | tf_op jit(solution)/shard_map/ppermute | solution.py:446
  26.1 0.1 collective-permute-start.12
  26.2 1.1 %collective-permute-start.13 = (bf16[1,528,256]{2,1,0:T(8,128)(2,1)S(1)}, bf16[1,528,256]{2,1,0:T(8,128)(2,1)S(1)}, u32[]{:S(2)}, u32[]{:S(2)}) collective-permute-start(bf16[1,528,256]{2,1,0:T(8,128)(2,1)S(1)} %collective-permute-done.5.refs_1_.refs_0_), channel_id=1, source_target_pairs={{0,2},{2,0},{4,6},{6,4},{8,10},{10,8},{12,14},{14,12},{16,18},{18,... | collective-permute-start | bytes 811016 | tf_op jit(solution)/shard_map/ppermute | solution.py:433
  27.3 0.0 collective-permute-start.14
  27.3 4.3 %attend.8.refs_2_ = f32[2,424,256]{2,1,0:T(8,128)S(1)} custom-call(bf16[2,272,256]{2,1,0:T(8,128)(2,1)S(1)} %stack.3.queries, bf16[8,528,256]{2,1,0:T(8,128)(2,1)S(1)} %get-tuple-element.46.refs_0_, bf16[2048,256]{1,0:T(8,128)(2,1)S(1)} %get-tuple-element.47.refs_1_), custom_call_target="tpu_custom_call" | custom-call | flops 2000000000 | bytes 1 | tf_op jit(solution)/shard_map/attend/pallas_call | solution.py:348
  31.6 0.0 collective-permute-done.13.refs_1_
  31.7 0.0 collective-permute-done.14.refs_3_
  31.7 0.4 gather.4
  32.1 2.6 %attend.9.refs_2_ = f32[2,424,256]{2,1,0:T(8,128)S(1)} custom-call(bf16[2,272,256]{2,1,0:T(8,128)(2,1)S(1)} %stack.2.queries, bf16[4,528,256]{2,1,0:T(8,128)(2,1)S(1)} %get-tuple-element.55.refs_0_, bf16[1024,256]{1,0:T(8,128)(2,1)S(1)} %get-tuple-element.56.refs_1_, f32[2,424,256]{2,1,0:T(8,128)S(1)} %attend.7.refs_2_), custom_call_target="tpu_custom_call" | custom-call | flops 1 | bytes 1 | tf_op jit(solution)/shard_map/attend/pallas_call | solution.py:348
  34.7 2.1 %collective-permute-done.12.refs_0_ = bf16[2,528,256]{2,1,0:T(8,128)(2,1)S(1)} collective-permute-done((bf16[2,528,256]{2,1,0:T(8,128)(2,1)S(1)}, bf16[2,528,256]{2,1,0:T(8,128)(2,1)S(1)}, u32[]{:S(2)}, u32[]{:S(2)}) %collective-permute-start.12) | collective-permute-done | bytes 540704 | tf_op jit(solution)/shard_map/ppermute | solution.py:452
  36.7 0.0 collective-permute-start.15
  36.7 2.6 %attend.10.refs_2_ = f32[2,424,256]{2,1,0:T(8,128)S(1)} custom-call(bf16[2,272,256]{2,1,0:T(8,128)(2,1)S(1)} %stack.3.queries, bf16[4,528,256]{2,1,0:T(8,128)(2,1)S(1)} %get-tuple-element.55.refs_0_, bf16[1024,256]{1,0:T(8,128)(2,1)S(1)} %get-tuple-element.56.refs_1_, f32[2,424,256]{2,1,0:T(8,128)S(1)} %attend.8.refs_2_), custom_call_target="tpu_custom_call" | custom-call | flops 2000000000 | bytes 1 | tf_op jit(solution)/shard_map/attend/pallas_call | solution.py:348
  39.4 0.0 collective-permute-done.15.refs_1_
  39.4 0.4 gather.5
  39.8 1.4 %attend.11 = s16[1,272,256]{2,1,0:T(8,128)(2,1)S(1)} custom-call(bf16[2,272,256]{2,1,0:T(8,128)(2,1)S(1)} %stack.3.queries, bf16[4,528,256]{2,1,0:T(8,128)(2,1)S(1)} %get-tuple-element.62.refs_0_, bf16[1024,256]{1,0:T(8,128)(2,1)S(1)} %get-tuple-element.63.refs_1_, f32[2,424,256]{2,1,0:T(8,128)S(1)} %attend.10.refs_2_), custom_call_target="tpu_custom_call" | custom-call | flops 1 | bytes 1 | tf_op jit(solution)/shard_map/attend/pallas_call | solution.py:348
  41.2 2.6 %collective-permute-start.16 = (s16[1,272,256]{2,1,0:T(8,128)(2,1)S(1)}, s16[1,272,256]{2,1,0:T(8,128)(2,1)S(1)}, u32[]{:S(2)}, u32[]{:S(2)}) collective-permute-start(s16[1,272,256]{2,1,0:T(8,128)(2,1)S(1)} %attend.11), channel_id=1, source_target_pairs={{32,0},{34,2},{36,4},{38,6},{40,8},{42,10},{44,12},{46,14},{48,16}... | collective-permute-start | bytes 417800 | tf_op jit(solution)/shard_map/ppermute | solution.py:466
  43.7 2.8 %attend.12 = (s16[1,272,256]{2,1,0:T(8,128)(2,1)S(1)}, s16[1,272,256]{2,1,0:T(8,128)(2,1)S(1)}) custom-call(bf16[2,272,256]{2,1,0:T(8,128)(2,1)S(1)} %stack.2.queries, bf16[4,528,256]{2,1,0:T(8,128)(2,1)S(1)} %get-tuple-element.62.refs_0_, bf16[1024,256]{1,0:T(8,128)(2,1)S(1)} %get-tuple-element.63.refs_1_, f32[2,424,256]{2,1,0:T(8,128)S(1)} %attend.9.refs_2_), custom_call_target="tpu_custom_call" | custom-call | flops 1 | bytes 1 | tf_op jit(solution)/shard_map/attend/pallas_call | solution.py:348
  46.6 0.7 %collective-permute-start.18 = (s16[1,272,256]{2,1,0:T(8,128)(2,1)S(1)}, s16[1,272,256]{2,1,0:T(8,128)(2,1)S(1)}, u32[]{:S(2)}, u32[]{:S(2)}) collective-permute-start(s16[1,272,256]{2,1,0:T(8,128)(2,1)S(1)} %get-tuple-element.70), channel_id=1, source_target_pairs={{48,0},{50,2},{52,4},{54,6},{56,8},{58,10},{60,12},{62,14},{0,16},... | collective-permute-start | bytes 417800 | tf_op jit(solution)/shard_map/ppermute | solution.py:469
  47.4 0.0 copy-start
  47.4 2.6 %collective-permute-start.17 = (s16[1,272,256]{2,1,0:T(8,128)(2,1)S(1)}, s16[1,272,256]{2,1,0:T(8,128)(2,1)S(1)}, u32[]{:S(2)}, u32[]{:S(2)}) collective-permute-start(s16[1,272,256]{2,1,0:T(8,128)(2,1)S(1)} %get-tuple-element.67), channel_id=1, source_target_pairs={{16,0},{18,2},{20,4},{22,6},{24,8},{26,10},{28,12},{30,14},{32,16}... | collective-permute-start | bytes 417800 | tf_op jit(solution)/shard_map/ppermute | solution.py:468
  49.9 0.0 collective-permute-done.16.refs_3_
  49.9 1.4 %attend.13.refs_0_ = s16[1,272,256]{2,1,0:T(8,128)(2,1)S(1)} custom-call(bf16[2,272,256]{2,1,0:T(8,128)(2,1)S(1)} %stack.3.queries, bf16[4,528,256]{2,1,0:T(8,128)(2,1)S(1)} %get-tuple-element.62.refs_0_, bf16[1024,256]{1,0:T(8,128)(2,1)S(1)} %get-tuple-element.63.refs_1_, f32[2,424,256]{2,1,0:T(8,128)S(1)} %attend.10.refs_2_), custom_call_target="tpu_custom_call" | custom-call | flops 1 | bytes 1 | tf_op jit(solution)/shard_map/attend/pallas_call | solution.py:348
  51.3 2.0 %collective-permute-done.18.refs_2_ = s16[1,272,256]{2,1,0:T(8,128)(2,1)S(1)} collective-permute-done((s16[1,272,256]{2,1,0:T(8,128)(2,1)S(1)}, s16[1,272,256]{2,1,0:T(8,128)(2,1)S(1)}, u32[]{:S(2)}, u32[]{:S(2)}) %collective-permute-start.18) | collective-permute-done | bytes 139296 | tf_op jit(solution)/shard_map/ppermute | solution.py:469
  53.3 0.0 collective-permute-done.17.refs_1_
  53.3 0.0 copy-done
  53.3 1.0 %combine.1 = (f32[256,128]{1,0:T(8,128)}, f32[256,128]{1,0:T(8,128)}) custom-call(s32[1,256]{1,0:T(1,128)S(1)} %bitcast.14, s16[1,272,256]{2,1,0:T(8,128)(2,1)S(1)} %attend.13.refs_0_, s16[1,272,256]{2,1,0:T(8,128)(2,1)S(1)} %collective-permute-done.17.refs_1_, s16[1,272,256]{2,1,0:T(8,128)(2,1)S(1)} %collective-permute-done.18.refs_2_, ...), custom_call_target="tpu_custom_call" | custom-call | flops 1 | bytes 1 | tf_op jit(solution)/shard_map/combine/pallas_call | solution.py:390
  (3 shorter events, 0.1 us)
Async XLA Ops:
  1.9 11.6 %collective-permute-start.4 = (bf16[1,528,256]{2,1,0:T(8,128)(2,1)S(1)}, bf16[1,528,256]{2,1,0:T(8,128)(2,1)S(1)}, u32[]{:S(2)}, u32[]{:S(2)}) collective-permute-start(bf16[1,528,256]{2,1,0:T(8,128)(2,1)S(1)} %bitcast.4), channel_id=1, source_target_pairs={{0,64},{2,66},{4,68},{6,70},{8,72},{10,74},{12,76},{14,78},{16,80}... | collective-permute-start | bytes 811016 | tf_op jit(solution)/shard_map/ppermute | solution.py:441
  3.6 9.9 %collective-permute-start.3 = (bf16[1,528,256]{2,1,0:T(8,128)(2,1)S(1)}, bf16[1,528,256]{2,1,0:T(8,128)(2,1)S(1)}, u32[]{:S(2)}, u32[]{:S(2)}) collective-permute-start(bf16[1,528,256]{2,1,0:T(8,128)(2,1)S(1)} %bitcast.5), channel_id=1, source_target_pairs={{0,4},{2,6},{4,8},{6,10},{8,12},{10,14},{12,0},{14,2},{16,20},{18,... | collective-permute-start | bytes 811016 | tf_op jit(solution)/shard_map/ppermute | solution.py:442
  5.1 8.4 %collective-permute-start.2 = (bf16[1,528,256]{2,1,0:T(8,128)(2,1)S(1)}, bf16[1,528,256]{2,1,0:T(8,128)(2,1)S(1)}, u32[]{:S(2)}, u32[]{:S(2)}) collective-permute-start(bf16[1,528,256]{2,1,0:T(8,128)(2,1)S(1)} %bitcast.6), channel_id=1, source_target_pairs={{0,12},{2,14},{4,0},{6,2},{8,4},{10,6},{12,8},{14,10},{16,28},{18,... | collective-permute-start | bytes 811016 | tf_op jit(solution)/shard_map/ppermute | solution.py:442
  6.8 6.3 %collective-permute-start.1 = (bf16[1,272,256]{2,1,0:T(8,128)(2,1)S(1)}, bf16[1,272,256]{2,1,0:T(8,128)(2,1)S(1)}, u32[]{:S(2)}, u32[]{:S(2)}) collective-permute-start(bf16[1,272,256]{2,1,0:T(8,128)(2,1)S(1)} %bitcast.9), channel_id=1, source_target_pairs={{0,16},{2,18},{4,20},{6,22},{8,24},{10,26},{12,28},{14,30},{16,32}... | collective-permute-start | bytes 417800 | tf_op jit(solution)/shard_map/ppermute | solution.py:443
  8.4 5.1 %collective-permute-start = (bf16[1,272,256]{2,1,0:T(8,128)(2,1)S(1)}, bf16[1,272,256]{2,1,0:T(8,128)(2,1)S(1)}, u32[]{:S(2)}, u32[]{:S(2)}) collective-permute-start(bf16[1,272,256]{2,1,0:T(8,128)(2,1)S(1)} %bitcast.10), channel_id=1, source_target_pairs={{0,48},{2,50},{4,52},{6,54},{8,56},{10,58},{12,60},{14,62},{16,0},... | collective-permute-start | bytes 417800 | tf_op jit(solution)/shard_map/ppermute | solution.py:443
  13.1 3.1 %collective-permute-start.8 = (bf16[1,528,256]{2,1,0:T(8,128)(2,1)S(1)}, bf16[1,528,256]{2,1,0:T(8,128)(2,1)S(1)}, u32[]{:S(2)}, u32[]{:S(2)}) collective-permute-start(bf16[1,528,256]{2,1,0:T(8,128)(2,1)S(1)} %bitcast.7), channel_id=1, source_target_pairs={{0,2},{2,0},{4,6},{6,4},{8,10},{10,8},{12,14},{14,12},{16,18},{18,... | collective-permute-start | bytes 811016 | tf_op jit(solution)/shard_map/ppermute | solution.py:433
  13.5 2.8 %collective-permute-start.10 = (bf16[1,528,256]{2,1,0:T(8,128)(2,1)S(1)}, bf16[1,528,256]{2,1,0:T(8,128)(2,1)S(1)}, u32[]{:S(2)}, u32[]{:S(2)}) collective-permute-start(bf16[1,528,256]{2,1,0:T(8,128)(2,1)S(1)} %collective-permute-done.3.refs_4_.refs_0_), channel_id=1, source_target_pairs={{0,2},{2,0},{4,6},{6,4},{8,10},{10,8},{12,14},{14,12},{16,18},{18,... | collective-permute-start | bytes 811016 | tf_op jit(solution)/shard_map/ppermute | solution.py:433
  13.7 5.8 %collective-permute-start.11 = (bf16[1,528,256]{2,1,0:T(8,128)(2,1)S(1)}, bf16[1,528,256]{2,1,0:T(8,128)(2,1)S(1)}, u32[]{:S(2)}, u32[]{:S(2)}) collective-permute-start(bf16[1,528,256]{2,1,0:T(8,128)(2,1)S(1)} %collective-permute-done.2.refs_6_.refs_2_), channel_id=1, source_target_pairs={{0,2},{2,0},{4,6},{6,4},{8,10},{10,8},{12,14},{14,12},{16,18},{18,... | collective-permute-start | bytes 811016 | tf_op jit(solution)/shard_map/ppermute | solution.py:433
  14.1 5.5 %collective-permute-start.9 = (bf16[1,528,256]{2,1,0:T(8,128)(2,1)S(1)}, bf16[1,528,256]{2,1,0:T(8,128)(2,1)S(1)}, u32[]{:S(2)}, u32[]{:S(2)}) collective-permute-start(bf16[1,528,256]{2,1,0:T(8,128)(2,1)S(1)} %collective-permute-done.4.refs_2_), channel_id=1, source_target_pairs={{0,2},{2,0},{4,6},{6,4},{8,10},{10,8},{12,14},{14,12},{16,18},{18,... | collective-permute-start | bytes 811016 | tf_op jit(solution)/shard_map/ppermute | solution.py:433
  14.2 10.4 %collective-permute-start.6 = (bf16[1,528,256]{2,1,0:T(8,128)(2,1)S(1)}, bf16[1,528,256]{2,1,0:T(8,128)(2,1)S(1)}, u32[]{:S(2)}, u32[]{:S(2)}) collective-permute-start(bf16[1,528,256]{2,1,0:T(8,128)(2,1)S(1)} %collective-permute-done.4.refs_2_), channel_id=1, source_target_pairs={{0,12},{2,14},{4,0},{6,2},{8,4},{10,6},{12,8},{14,10},{16,28},{18,... | collective-permute-start | bytes 811016 | tf_op jit(solution)/shard_map/ppermute | solution.py:446
  16.2 9.8 %collective-permute-start.5 = (bf16[1,528,256]{2,1,0:T(8,128)(2,1)S(1)}, bf16[1,528,256]{2,1,0:T(8,128)(2,1)S(1)}, u32[]{:S(2)}, u32[]{:S(2)}) collective-permute-start(bf16[1,528,256]{2,1,0:T(8,128)(2,1)S(1)} %collective-permute-done.4.refs_2_), channel_id=1, source_target_pairs={{0,4},{2,6},{4,8},{6,10},{8,12},{10,14},{12,0},{14,2},{16,20},{18,... | collective-permute-start | bytes 811016 | tf_op jit(solution)/shard_map/ppermute | solution.py:446
  16.3 8.4 %collective-permute-start.7 = (bf16[1,272,256]{2,1,0:T(8,128)(2,1)S(1)}, bf16[1,272,256]{2,1,0:T(8,128)(2,1)S(1)}, u32[]{:S(2)}, u32[]{:S(2)}) collective-permute-start(bf16[1,272,256]{2,1,0:T(8,128)(2,1)S(1)} %bitcast.11), channel_id=1, source_target_pairs={{0,32},{2,34},{4,36},{6,38},{8,40},{10,42},{12,44},{14,46},{16,48}... | collective-permute-start | bytes 417800 | tf_op jit(solution)/shard_map/ppermute | solution.py:445
  26.1 10.6 %collective-permute-start.12 = (bf16[2,528,256]{2,1,0:T(8,128)(2,1)S(1)}, bf16[2,528,256]{2,1,0:T(8,128)(2,1)S(1)}, u32[]{:S(2)}, u32[]{:S(2)}) collective-permute-start(bf16[2,528,256]{2,1,0:T(8,128)(2,1)S(1)} %choose.1), channel_id=1, source_target_pairs={{0,4},{2,14},{4,8},{6,2},{8,12},{10,6},{12,0},{14,10},{16,20},{18,... | collective-permute-start | bytes 1622024 | tf_op jit(solution)/shard_map/ppermute | solution.py:452
  26.2 5.5 %collective-permute-start.13 = (bf16[1,528,256]{2,1,0:T(8,128)(2,1)S(1)}, bf16[1,528,256]{2,1,0:T(8,128)(2,1)S(1)}, u32[]{:S(2)}, u32[]{:S(2)}) collective-permute-start(bf16[1,528,256]{2,1,0:T(8,128)(2,1)S(1)} %collective-permute-done.5.refs_1_.refs_0_), channel_id=1, source_target_pairs={{0,2},{2,0},{4,6},{6,4},{8,10},{10,8},{12,14},{14,12},{16,18},{18,... | collective-permute-start | bytes 811016 | tf_op jit(solution)/shard_map/ppermute | solution.py:433
  27.3 4.4 %collective-permute-start.14 = (bf16[1,528,256]{2,1,0:T(8,128)(2,1)S(1)}, bf16[1,528,256]{2,1,0:T(8,128)(2,1)S(1)}, u32[]{:S(2)}, u32[]{:S(2)}) collective-permute-start(bf16[1,528,256]{2,1,0:T(8,128)(2,1)S(1)} %collective-permute-done.6.refs_3_.refs_2_), channel_id=1, source_target_pairs={{0,2},{2,0},{4,6},{6,4},{8,10},{10,8},{12,14},{14,12},{16,18},{18,... | collective-permute-start | bytes 811016 | tf_op jit(solution)/shard_map/ppermute | solution.py:433
  36.7 2.6 %collective-permute-start.15 = (bf16[2,528,256]{2,1,0:T(8,128)(2,1)S(1)}, bf16[2,528,256]{2,1,0:T(8,128)(2,1)S(1)}, u32[]{:S(2)}, u32[]{:S(2)}) collective-permute-start(bf16[2,528,256]{2,1,0:T(8,128)(2,1)S(1)} %collective-permute-done.12.refs_0_), channel_id=1, source_target_pairs={{0,2},{2,0},{4,6},{6,4},{8,10},{10,8},{12,14},{14,12},{16,18},{18,... | collective-permute-start | bytes 1622024 | tf_op jit(solution)/shard_map/ppermute | solution.py:433
  41.2 8.7 %collective-permute-start.16 = (s16[1,272,256]{2,1,0:T(8,128)(2,1)S(1)}, s16[1,272,256]{2,1,0:T(8,128)(2,1)S(1)}, u32[]{:S(2)}, u32[]{:S(2)}) collective-permute-start(s16[1,272,256]{2,1,0:T(8,128)(2,1)S(1)} %attend.11), channel_id=1, source_target_pairs={{32,0},{34,2},{36,4},{38,6},{40,8},{42,10},{44,12},{46,14},{48,16}... | collective-permute-start | bytes 417800 | tf_op jit(solution)/shard_map/ppermute | solution.py:466
  46.6 6.7 %collective-permute-start.18 = (s16[1,272,256]{2,1,0:T(8,128)(2,1)S(1)}, s16[1,272,256]{2,1,0:T(8,128)(2,1)S(1)}, u32[]{:S(2)}, u32[]{:S(2)}) collective-permute-start(s16[1,272,256]{2,1,0:T(8,128)(2,1)S(1)} %get-tuple-element.70), channel_id=1, source_target_pairs={{48,0},{50,2},{52,4},{54,6},{56,8},{58,10},{60,12},{62,14},{0,16},... | collective-permute-start | bytes 417800 | tf_op jit(solution)/shard_map/ppermute | solution.py:469
  47.4 6.0 %copy-start = (s32[256]{0:T(256)S(1)}, s32[256]{0:T(256)}, u32[]{:S(2)}) copy-start(s32[256]{0:T(256)} %param.13) | copy-start | bytes 3076
  47.4 6.0 %collective-permute-start.17 = (s16[1,272,256]{2,1,0:T(8,128)(2,1)S(1)}, s16[1,272,256]{2,1,0:T(8,128)(2,1)S(1)}, u32[]{:S(2)}, u32[]{:S(2)}) collective-permute-start(s16[1,272,256]{2,1,0:T(8,128)(2,1)S(1)} %get-tuple-element.67), channel_id=1, source_target_pairs={{16,0},{18,2},{20,4},{22,6},{24,8},{26,10},{28,12},{30,14},{32,16}... | collective-permute-start | bytes 417800 | tf_op jit(solution)/shard_map/ppermute | solution.py:468

commit v2 on v1

--- a/solution.py
+++ b/solution.py
@@ -23,8 +23,8 @@
 STATE_ROWS = 424
 FULL = 32767.0
 VMEM = pl.BlockSpec(memory_space=pltpu.VMEM)
-WAITED = pl.CostEstimate(flops=2 * 10**9, bytes_accessed=1, transcendentals=0)
-LIGHT = pl.CostEstimate(flops=1, bytes_accessed=1, transcendentals=0)
+WAITED = pl.CostEstimate(flops=2 * 10**9, bytes_accessed=2**21, transcendentals=0)
+LIGHT = pl.CostEstimate(flops=1, bytes_accessed=2**21, transcendentals=0)
 SMALL = pltpu.CompilerParams(vmem_limit_bytes=8 * 2**20)
 LARGE = pltpu.CompilerParams(vmem_limit_bytes=16 * 2**20)
 
@@ -443,14 +443,15 @@
     q_next, q_last = move(q, perm=Q_NEXT), move(q, perm=Q_LAST)
     q_last, q_next, left, right, level = together(q_last, q_next, left, right, level)
     q_far = move(q, perm=Q_FAR)
-    level_right, level_left = move(level, perm=RIGHT), move(level, perm=LEFT)
-    first = gather(*both(kv), *both(level), *both(right), *both(left))
+    level_pair = stack(*both(level), counts=(1, 1))
+    level_near = move(level_pair, perm=BOTH_WAYS)
+    first = gather(*both(kv), level_pair, *both(right), *both(left))
     near_held = stack(q_last, q_next, counts=(1, 1))
     near_state = attend(near_held, first)
 
-    level_right, level_left, q_far, near_state = together(level_right, level_left, q_far, near_state)
-    on = move(choose(core, (right, level_right), (left, level_left)), perm=BOTH_WAYS)
-    more = both(level_right) + both(level_left)
+    level_near, q_far, near_state = together(level_near, q_far, near_state)
+    on = move(choose(core, (right, level_near), (left, level_near)), perm=BOTH_WAYS)
+    more = both(level_near)
     held = stack(q_far, q, counts=(1, 1))
     state = attend(held, first, expect=WAITED)
     *more, state = together(*more, state)

time: 54.7 us -> 54.4 us (level)
  Pallas kernels: 23.3 us -> 19.8 us
  waiting for transfers between devices: 8.88 us -> 11.5 us
  local copies, waits for them, and re-layouts: 0.01 us -> 1.38 us
  starting transfers between devices: 21.3 us -> 20.2 us
    pallas_call x7, Pallas kernels: 19.5 us -> 14.9 us  [attend(): pl.pallas_call(kernel, out_shape=out_shape, in_specs=[VMEM] * len(operand...]
    ppermute x7 -> x6, waiting for transfers between devices: 0.02 us -> 3.14 us  [sibling(): return move(group, perm=SIBLING)]
    unnamed x2 -> x6, local copies, waits for them, and re-layouts: 0.01 us -> 1.38 us
    ppermute x3 -> x2, starting transfers between devices: 2.1 us -> 0.9 us  [the longest x1 0.75 us: per_device(): level_near = move(level_pair, perm=BOTH_WAYS)]
    pallas_call x3, Pallas kernels: 1.5 us -> 2.54 us  [gather(): pl.pallas_call(gather_kernel, out_shape=(jax.ShapeDtypeStruct((blocks, KV...]
    ppermute x3 -> x2, waiting for transfers between devices: 3.47 us -> 2.99 us  [the longest x1 2.99 us: per_device(): move(choose(core, (right, level_near), (left, level_near)), perm=BOTH_WAYS)]
    ppermute x7 -> x6, starting transfers between devices: 1.87 us -> 2.01 us  [sibling(): return move(group, perm=SIBLING)]
  transfers between devices with their start and end apart: 19 -> 17, of which waited for: 5 -> 6; matrix products, arithmetic and copies ran while one was open for 0% -> 0% of each run, Pallas kernels for 35% -> 29%
where the time goes in v2:
time: 54.4 us; the launch traced here: 53.8 us
  starting transfers between devices  20.2 us (37%)
  Pallas kernels  19.8 us (36%)
  waiting for transfers between devices  11.5 us (21%)
  local copies, waits for them, and re-layouts  1.38 us (3%)
  between operations  0.84 us (2%)
    pallas_call x7, Pallas kernels, attend(): pl.pallas_call(kernel, out_shape=out_shape, in_specs=[VMEM] * len(operand...  14.9 us
    ppermute x2, waiting for transfers between devices, per_device(): q_next, q_last = (move(q, perm=Q_NEXT), move(q, perm=Q_LAST))  3.39 us
    ppermute x2, starting transfers between devices, per_device(): q_next, q_last = (move(q, perm=Q_NEXT), move(q, perm=Q_LAST))  3.24 us
    ppermute x2, starting transfers between devices, per_device(): right, left = (move(kv, perm=RIGHT), move(kv, perm=LEFT))  3.24 us
    ppermute x1, starting transfers between devices, per_device(): q_far = move(q, perm=Q_FAR)  3.19 us
    ppermute x6, waiting for transfers between devices, sibling(): return move(group, perm=SIBLING)  3.14 us
    ppermute x1, waiting for transfers between devices, per_device(): move(choose(core, (right, level_near), (left, level_near)), perm=BOTH_WAYS)  2.99 us
    ppermute x1, starting transfers between devices, per_device(): back_far = move(out_far, perm=back(Q_FAR))  2.58 us
  transfers between devices with their start and end apart: 17, of which 6 were waited for; matrix products, arithmetic and copies ran while one was open for 0% of the time, Pallas kernels for 29%

profile of v2, /device:TPU:64, one launch (start us, length us, event | category | flops | bytes accessed | tf_op | source)
XLA Modules:
  0.0 53.8 jit_solution(4136931651806112847)
XLA Ops:
  0.6 1.3 %pack.1 = (bf16[528,256]{1,0:T(8,128)(2,1)S(1)}, bf16[272,256]{1,0:T(8,128)(2,1)S(1)}) custom-call(bf16[256,128]{1,0:T(8,128)(2,1)} %refs_0_.1, bf16[256,128]{1,0:T(8,128)(2,1)} %refs_1_.1, bf16[256,128]{1,0:T(8,128)(2,1)} %refs_2_.1, bf16[256,128]{1,0:T(8,128)(2,1)} %refs_3_.1, bf16[256,128]{1,0:T(8,128)(2,1)} %refs_4_.1, bf16[256,128]{1,0:T(8,128)(2,1)} %refs_5_.1, ...), custom_call_target="tpu_custom_call" | custom-call | flops 1 | bytes 2097152 | tf_op jit(solution)/shard_map/pack/pallas_call | solution.py:64
  1.9 1.7 %collective-permute-start.4 = (bf16[1,528,256]{2,1,0:T(8,128)(2,1)S(1)}, bf16[1,528,256]{2,1,0:T(8,128)(2,1)S(1)}, u32[]{:S(2)}, u32[]{:S(2)}) collective-permute-start(bf16[1,528,256]{2,1,0:T(8,128)(2,1)S(1)} %bitcast.4), channel_id=1, source_target_pairs={{0,64},{2,66},{4,68},{6,70},{8,72},{10,74},{12,76},{14,78},{16,80}... | collective-permute-start | bytes 811016 | tf_op jit(solution)/shard_map/ppermute | solution.py:441
  3.6 1.5 %collective-permute-start.3 = (bf16[1,528,256]{2,1,0:T(8,128)(2,1)S(1)}, bf16[1,528,256]{2,1,0:T(8,128)(2,1)S(1)}, u32[]{:S(2)}, u32[]{:S(2)}) collective-permute-start(bf16[1,528,256]{2,1,0:T(8,128)(2,1)S(1)} %bitcast.5), channel_id=1, source_target_pairs={{0,4},{2,6},{4,8},{6,10},{8,12},{10,14},{12,0},{14,2},{16,20},{18,... | collective-permute-start | bytes 811016 | tf_op jit(solution)/shard_map/ppermute | solution.py:442
  5.1 1.7 %collective-permute-start.2 = (bf16[1,528,256]{2,1,0:T(8,128)(2,1)S(1)}, bf16[1,528,256]{2,1,0:T(8,128)(2,1)S(1)}, u32[]{:S(2)}, u32[]{:S(2)}) collective-permute-start(bf16[1,528,256]{2,1,0:T(8,128)(2,1)S(1)} %bitcast.6), channel_id=1, source_target_pairs={{0,12},{2,14},{4,0},{6,2},{8,4},{10,6},{12,8},{14,10},{16,28},{18,... | collective-permute-start | bytes 811016 | tf_op jit(solution)/shard_map/ppermute | solution.py:442
  6.8 1.6 %collective-permute-start.1 = (bf16[1,272,256]{2,1,0:T(8,128)(2,1)S(1)}, bf16[1,272,256]{2,1,0:T(8,128)(2,1)S(1)}, u32[]{:S(2)}, u32[]{:S(2)}) collective-permute-start(bf16[1,272,256]{2,1,0:T(8,128)(2,1)S(1)} %bitcast.9), channel_id=1, source_target_pairs={{0,16},{2,18},{4,20},{6,22},{8,24},{10,26},{12,28},{14,30},{16,32}... | collective-permute-start | bytes 417800 | tf_op jit(solution)/shard_map/ppermute | solution.py:443
  8.4 1.7 %collective-permute-start = (bf16[1,272,256]{2,1,0:T(8,128)(2,1)S(1)}, bf16[1,272,256]{2,1,0:T(8,128)(2,1)S(1)}, u32[]{:S(2)}, u32[]{:S(2)}) collective-permute-start(bf16[1,272,256]{2,1,0:T(8,128)(2,1)S(1)} %bitcast.10), channel_id=1, source_target_pairs={{0,48},{2,50},{4,52},{6,54},{8,56},{10,58},{12,60},{14,62},{16,0},... | collective-permute-start | bytes 417800 | tf_op jit(solution)/shard_map/ppermute | solution.py:443
  10.1 3.0 %collective-permute-done.1.refs_1_ = bf16[1,272,256]{2,1,0:T(8,128)(2,1)S(1)} collective-permute-done((bf16[1,272,256]{2,1,0:T(8,128)(2,1)S(1)}, bf16[1,272,256]{2,1,0:T(8,128)(2,1)S(1)}, u32[]{:S(2)}, u32[]{:S(2)}) %collective-permute-start.1) | collective-permute-done | bytes 139296 | tf_op jit(solution)/shard_map/ppermute | solution.py:443
  13.1 0.4 collective-permute-done.refs_0_
  13.5 0.0 collective-permute-done.4.refs_0_
  13.5 0.0 collective-permute-done.3.refs_3_.refs_0_
  13.5 0.0 collective-permute-done.2.refs_5_.refs_2_
  13.5 0.1 collective-permute-start.5
  13.6 1.5 %collective-permute-done.5.refs_1_ = bf16[1,528,256]{2,1,0:T(8,128)(2,1)S(1)} collective-permute-done((bf16[1,528,256]{2,1,0:T(8,128)(2,1)S(1)}, bf16[1,528,256]{2,1,0:T(8,128)(2,1)S(1)}, u32[]{:S(2)}, u32[]{:S(2)}) %collective-permute-start.5) | collective-permute-done | bytes 270368 | tf_op jit(solution)/shard_map/ppermute | solution.py:433
  15.1 0.8 %collective-permute-start.6 = (bf16[2,528,256]{2,1,0:T(8,128)(2,1)S(1)}, bf16[2,528,256]{2,1,0:T(8,128)(2,1)S(1)}, u32[]{:S(2)}, u32[]{:S(2)}) collective-permute-start(bf16[2,528,256]{2,1,0:T(8,128)(2,1)S(1)} %stack.3.refs_2_), channel_id=1, source_target_pairs={{0,4},{2,14},{4,8},{6,2},{8,12},{10,6},{12,0},{14,10},{16,20},{18,... | collective-permute-start | bytes 1622024 | tf_op jit(solution)/shard_map/ppermute | solution.py:447
  15.9 1.3 %collective-permute-start.8 = (bf16[1,528,256]{2,1,0:T(8,128)(2,1)S(1)}, bf16[1,528,256]{2,1,0:T(8,128)(2,1)S(1)}, u32[]{:S(2)}, u32[]{:S(2)}) collective-permute-start(bf16[1,528,256]{2,1,0:T(8,128)(2,1)S(1)} %bitcast.7), channel_id=1, source_target_pairs={{0,2},{2,0},{4,6},{6,4},{8,10},{10,8},{12,14},{14,12},{16,18},{18,... | collective-permute-start | bytes 811016 | tf_op jit(solution)/shard_map/ppermute | solution.py:433
  17.2 0.0 collective-permute-start.9
  17.2 0.5 collective-permute-start.10
  17.7 3.2 %collective-permute-start.7 = (bf16[1,272,256]{2,1,0:T(8,128)(2,1)S(1)}, bf16[1,272,256]{2,1,0:T(8,128)(2,1)S(1)}, u32[]{:S(2)}, u32[]{:S(2)}) collective-permute-start(bf16[1,272,256]{2,1,0:T(8,128)(2,1)S(1)} %bitcast.11), channel_id=1, source_target_pairs={{0,32},{2,34},{4,36},{6,38},{8,40},{10,42},{12,44},{14,46},{16,48}... | collective-permute-start | bytes 417800 | tf_op jit(solution)/shard_map/ppermute | solution.py:445
  20.9 0.0 collective-permute-done.8.refs_1_
  21.0 0.0 collective-permute-done.9.refs_4_
  21.0 0.0 collective-permute-done.10.refs_6_
  21.0 0.7 %gather.3 = (bf16[8,528,256]{2,1,0:T(8,128)(2,1)S(1)}, bf16[2048,256]{1,0:T(8,128)(2,1)S(1)}) custom-call(bf16[1,528,256]{2,1,0:T(8,128)(2,1)S(1)} %bitcast.8, bf16[1,528,256]{2,1,0:T(8,128)(2,1)S(1)} %collective-permute-done.8.refs_1_, bf16[2,528,256]{2,1,0:T(8,128)(2,1)S(1)} %stack.3.refs_2_, ...), custom_call_target="tpu_custom_call" | custom-call | flops 1 | bytes 2097152 | tf_op jit(solution)/shard_map/gather/pallas_call | solution.py:183
  21.7 0.0 copy-start
  21.7 4.3 %attend.7.refs_2_ = f32[2,424,256]{2,1,0:T(8,128)S(1)} custom-call(bf16[2,272,256]{2,1,0:T(8,128)(2,1)S(1)} %stack.4.queries, bf16[8,528,256]{2,1,0:T(8,128)(2,1)S(1)} %get-tuple-element.43.refs_0_, bf16[2048,256]{1,0:T(8,128)(2,1)S(1)} %get-tuple-element.44.refs_1_), custom_call_target="tpu_custom_call" | custom-call | flops 1 | bytes 2097152 | tf_op jit(solution)/shard_map/attend/pallas_call | solution.py:348
  26.0 0.0 copy-done
  26.1 0.0 collective-permute-done.7.refs_0_
  26.1 0.0 collective-permute-done.6.refs_1_.refs_3_.refs_0_
  26.1 0.1 collective-permute-start.12
  26.2 0.0 copy-start.1
  26.2 0.2 collective-permute-start.11
  26.4 1.4 %copy-done.1 = bf16[8,528,256]{2,1,0:T(8,128)(2,1)S(1)} copy-done((bf16[8,528,256]{2,1,0:T(8,128)(2,1)S(1)}, bf16[8,528,256]{2,1,0:T(8,128)(2,1)}, u32[]{:S(2)}) %copy-start.1) | copy-done | bytes 2162712
  27.8 4.3 %attend.8.refs_2_ = f32[2,424,256]{2,1,0:T(8,128)S(1)} custom-call(bf16[2,272,256]{2,1,0:T(8,128)(2,1)S(1)} %stack.5.queries, bf16[8,528,256]{2,1,0:T(8,128)(2,1)S(1)} %copy-done.1, bf16[2048,256]{1,0:T(8,128)(2,1)S(1)} %get-tuple-element.44.refs_1_), custom_call_target="tpu_custom_call" | custom-call | flops 2000000000 | bytes 2097152 | tf_op jit(solution)/shard_map/attend/pallas_call | solution.py:348
  32.1 0.0 collective-permute-done.12.refs_1_
  32.1 1.4 %gather.4 = (bf16[4,528,256]{2,1,0:T(8,128)(2,1)S(1)}, bf16[1024,256]{1,0:T(8,128)(2,1)S(1)}) custom-call(bf16[2,528,256]{2,1,0:T(8,128)(2,1)S(1)} %collective-permute-done.6.refs_1_.refs_3_.refs_0_, bf16[2,528,256]{2,1,0:T(8,128)(2,1)} %collective-permute-done.12.refs_1_), custom_call_target="tpu_custom_call" | custom-call | flops 1 | bytes 2097152 | tf_op jit(solution)/shard_map/gather/pallas_call | solution.py:183
  33.5 0.3 attend.9.refs_2_
  33.9 3.0 %collective-permute-done.11.refs_0_ = bf16[2,528,256]{2,1,0:T(8,128)(2,1)S(1)} collective-permute-done((bf16[2,528,256]{2,1,0:T(8,128)(2,1)S(1)}, bf16[2,528,256]{2,1,0:T(8,128)(2,1)S(1)}, u32[]{:S(2)}, u32[]{:S(2)}) %collective-permute-start.11) | collective-permute-done | bytes 540704 | tf_op jit(solution)/shard_map/ppermute | solution.py:453
  36.9 0.0 collective-permute-start.13
  36.9 0.3 attend.10.refs_2_
  37.2 1.6 %collective-permute-done.13.refs_1_ = bf16[2,528,256]{2,1,0:T(8,128)(2,1)S(1)} collective-permute-done((bf16[2,528,256]{2,1,0:T(8,128)(2,1)S(1)}, bf16[2,528,256]{2,1,0:T(8,128)(2,1)S(1)}, u32[]{:S(2)}, u32[]{:S(2)}) %collective-permute-start.13) | collective-permute-done | bytes 540704 | tf_op jit(solution)/shard_map/ppermute | solution.py:433
  38.8 0.4 gather.5
  39.2 1.4 %attend.11 = s16[1,272,256]{2,1,0:T(8,128)(2,1)S(1)} custom-call(bf16[2,272,256]{2,1,0:T(8,128)(2,1)S(1)} %stack.5.queries, bf16[4,528,256]{2,1,0:T(8,128)(2,1)S(1)} %get-tuple-element.56.refs_0_, bf16[1024,256]{1,0:T(8,128)(2,1)S(1)} %get-tuple-element.57.refs_1_, f32[2,424,256]{2,1,0:T(8,128)S(1)} %attend.10.refs_2_), custom_call_target="tpu_custom_call" | custom-call | flops 1 | bytes 2097152 | tf_op jit(solution)/shard_map/attend/pallas_call | solution.py:348
  40.6 2.6 %collective-permute-start.14 = (s16[1,272,256]{2,1,0:T(8,128)(2,1)S(1)}, s16[1,272,256]{2,1,0:T(8,128)(2,1)S(1)}, u32[]{:S(2)}, u32[]{:S(2)}) collective-permute-start(s16[1,272,256]{2,1,0:T(8,128)(2,1)S(1)} %attend.11), channel_id=1, source_target_pairs={{32,0},{34,2},{36,4},{38,6},{40,8},{42,10},{44,12},{46,14},{48,16}... | collective-permute-start | bytes 417800 | tf_op jit(solution)/shard_map/ppermute | solution.py:467
  43.2 2.8 %attend.12 = (s16[1,272,256]{2,1,0:T(8,128)(2,1)S(1)}, s16[1,272,256]{2,1,0:T(8,128)(2,1)S(1)}) custom-call(bf16[2,272,256]{2,1,0:T(8,128)(2,1)S(1)} %stack.4.queries, bf16[4,528,256]{2,1,0:T(8,128)(2,1)S(1)} %get-tuple-element.56.refs_0_, bf16[1024,256]{1,0:T(8,128)(2,1)S(1)} %get-tuple-element.57.refs_1_, f32[2,424,256]{2,1,0:T(8,128)S(1)} %attend.9.refs_2_), custom_call_target="tpu_custom_call" | custom-call | flops 1 | bytes 2097152 | tf_op jit(solution)/shard_map/attend/pallas_call | solution.py:348
  46.1 0.9 %collective-permute-start.16 = (s16[1,272,256]{2,1,0:T(8,128)(2,1)S(1)}, s16[1,272,256]{2,1,0:T(8,128)(2,1)S(1)}, u32[]{:S(2)}, u32[]{:S(2)}) collective-permute-start(s16[1,272,256]{2,1,0:T(8,128)(2,1)S(1)} %get-tuple-element.64), channel_id=1, source_target_pairs={{48,0},{50,2},{52,4},{54,6},{56,8},{58,10},{60,12},{62,14},{0,16},... | collective-permute-start | bytes 417800 | tf_op jit(solution)/shard_map/ppermute | solution.py:470
  46.9 0.0 copy-start.2
  46.9 2.4 %collective-permute-start.15 = (s16[1,272,256]{2,1,0:T(8,128)(2,1)S(1)}, s16[1,272,256]{2,1,0:T(8,128)(2,1)S(1)}, u32[]{:S(2)}, u32[]{:S(2)}) collective-permute-start(s16[1,272,256]{2,1,0:T(8,128)(2,1)S(1)} %get-tuple-element.61), channel_id=1, source_target_pairs={{16,0},{18,2},{20,4},{22,6},{24,8},{26,10},{28,12},{30,14},{32,16}... | collective-permute-start | bytes 417800 | tf_op jit(solution)/shard_map/ppermute | solution.py:469
  49.4 0.0 collective-permute-done.14.refs_3_
  49.4 1.4 %attend.13.refs_0_ = s16[1,272,256]{2,1,0:T(8,128)(2,1)S(1)} custom-call(bf16[2,272,256]{2,1,0:T(8,128)(2,1)S(1)} %stack.5.queries, bf16[4,528,256]{2,1,0:T(8,128)(2,1)S(1)} %get-tuple-element.56.refs_0_, bf16[1024,256]{1,0:T(8,128)(2,1)S(1)} %get-tuple-element.57.refs_1_, f32[2,424,256]{2,1,0:T(8,128)S(1)} %attend.10.refs_2_), custom_call_target="tpu_custom_call" | custom-call | flops 1 | bytes 2097152 | tf_op jit(solution)/shard_map/attend/pallas_call | solution.py:348
  50.8 2.0 %collective-permute-done.16.refs_2_ = s16[1,272,256]{2,1,0:T(8,128)(2,1)S(1)} collective-permute-done((s16[1,272,256]{2,1,0:T(8,128)(2,1)S(1)}, s16[1,272,256]{2,1,0:T(8,128)(2,1)S(1)}, u32[]{:S(2)}, u32[]{:S(2)}) %collective-permute-start.16) | collective-permute-done | bytes 139296 | tf_op jit(solution)/shard_map/ppermute | solution.py:470
  52.8 0.0 collective-permute-done.15.refs_1_
  52.8 0.0 copy-done.2
  52.8 1.0 %combine.1 = (f32[256,128]{1,0:T(8,128)}, f32[256,128]{1,0:T(8,128)}) custom-call(s32[1,256]{1,0:T(1,128)S(1)} %bitcast.14, s16[1,272,256]{2,1,0:T(8,128)(2,1)S(1)} %attend.13.refs_0_, s16[1,272,256]{2,1,0:T(8,128)(2,1)S(1)} %collective-permute-done.15.refs_1_, s16[1,272,256]{2,1,0:T(8,128)(2,1)S(1)} %collective-permute-done.16.refs_2_, ...), custom_call_target="tpu_custom_call" | custom-call | flops 1 | bytes 2097152 | tf_op jit(solution)/shard_map/combine/pallas_call | solution.py:390
  (4 shorter events, 0.1 us)
Async XLA Ops:
  1.9 11.6 %collective-permute-start.4 = (bf16[1,528,256]{2,1,0:T(8,128)(2,1)S(1)}, bf16[1,528,256]{2,1,0:T(8,128)(2,1)S(1)}, u32[]{:S(2)}, u32[]{:S(2)}) collective-permute-start(bf16[1,528,256]{2,1,0:T(8,128)(2,1)S(1)} %bitcast.4), channel_id=1, source_target_pairs={{0,64},{2,66},{4,68},{6,70},{8,72},{10,74},{12,76},{14,78},{16,80}... | collective-permute-start | bytes 811016 | tf_op jit(solution)/shard_map/ppermute | solution.py:441
  3.6 9.9 %collective-permute-start.3 = (bf16[1,528,256]{2,1,0:T(8,128)(2,1)S(1)}, bf16[1,528,256]{2,1,0:T(8,128)(2,1)S(1)}, u32[]{:S(2)}, u32[]{:S(2)}) collective-permute-start(bf16[1,528,256]{2,1,0:T(8,128)(2,1)S(1)} %bitcast.5), channel_id=1, source_target_pairs={{0,4},{2,6},{4,8},{6,10},{8,12},{10,14},{12,0},{14,2},{16,20},{18,... | collective-permute-start | bytes 811016 | tf_op jit(solution)/shard_map/ppermute | solution.py:442
  5.1 8.4 %collective-permute-start.2 = (bf16[1,528,256]{2,1,0:T(8,128)(2,1)S(1)}, bf16[1,528,256]{2,1,0:T(8,128)(2,1)S(1)}, u32[]{:S(2)}, u32[]{:S(2)}) collective-permute-start(bf16[1,528,256]{2,1,0:T(8,128)(2,1)S(1)} %bitcast.6), channel_id=1, source_target_pairs={{0,12},{2,14},{4,0},{6,2},{8,4},{10,6},{12,8},{14,10},{16,28},{18,... | collective-permute-start | bytes 811016 | tf_op jit(solution)/shard_map/ppermute | solution.py:442
  6.8 6.3 %collective-permute-start.1 = (bf16[1,272,256]{2,1,0:T(8,128)(2,1)S(1)}, bf16[1,272,256]{2,1,0:T(8,128)(2,1)S(1)}, u32[]{:S(2)}, u32[]{:S(2)}) collective-permute-start(bf16[1,272,256]{2,1,0:T(8,128)(2,1)S(1)} %bitcast.9), channel_id=1, source_target_pairs={{0,16},{2,18},{4,20},{6,22},{8,24},{10,26},{12,28},{14,30},{16,32}... | collective-permute-start | bytes 417800 | tf_op jit(solution)/shard_map/ppermute | solution.py:443
  8.4 5.1 %collective-permute-start = (bf16[1,272,256]{2,1,0:T(8,128)(2,1)S(1)}, bf16[1,272,256]{2,1,0:T(8,128)(2,1)S(1)}, u32[]{:S(2)}, u32[]{:S(2)}) collective-permute-start(bf16[1,272,256]{2,1,0:T(8,128)(2,1)S(1)} %bitcast.10), channel_id=1, source_target_pairs={{0,48},{2,50},{4,52},{6,54},{8,56},{10,58},{12,60},{14,62},{16,0},... | collective-permute-start | bytes 417800 | tf_op jit(solution)/shard_map/ppermute | solution.py:443
  13.5 1.6 %collective-permute-start.5 = (bf16[1,528,256]{2,1,0:T(8,128)(2,1)S(1)}, bf16[1,528,256]{2,1,0:T(8,128)(2,1)S(1)}, u32[]{:S(2)}, u32[]{:S(2)}) collective-permute-start(bf16[1,528,256]{2,1,0:T(8,128)(2,1)S(1)} %collective-permute-done.4.refs_0_), channel_id=1, source_target_pairs={{0,2},{2,0},{4,6},{6,4},{8,10},{10,8},{12,14},{14,12},{16,18},{18,... | collective-permute-start | bytes 811016 | tf_op jit(solution)/shard_map/ppermute | solution.py:433
  15.1 10.9 %collective-permute-start.6 = (bf16[2,528,256]{2,1,0:T(8,128)(2,1)S(1)}, bf16[2,528,256]{2,1,0:T(8,128)(2,1)S(1)}, u32[]{:S(2)}, u32[]{:S(2)}) collective-permute-start(bf16[2,528,256]{2,1,0:T(8,128)(2,1)S(1)} %stack.3.refs_2_), channel_id=1, source_target_pairs={{0,4},{2,14},{4,8},{6,2},{8,12},{10,6},{12,0},{14,10},{16,20},{18,... | collective-permute-start | bytes 1622024 | tf_op jit(solution)/shard_map/ppermute | solution.py:447
  15.9 5.1 %collective-permute-start.8 = (bf16[1,528,256]{2,1,0:T(8,128)(2,1)S(1)}, bf16[1,528,256]{2,1,0:T(8,128)(2,1)S(1)}, u32[]{:S(2)}, u32[]{:S(2)}) collective-permute-start(bf16[1,528,256]{2,1,0:T(8,128)(2,1)S(1)} %bitcast.7), channel_id=1, source_target_pairs={{0,2},{2,0},{4,6},{6,4},{8,10},{10,8},{12,14},{14,12},{16,18},{18,... | collective-permute-start | bytes 811016 | tf_op jit(solution)/shard_map/ppermute | solution.py:433
  17.2 3.7 %collective-permute-start.9 = (bf16[1,528,256]{2,1,0:T(8,128)(2,1)S(1)}, bf16[1,528,256]{2,1,0:T(8,128)(2,1)S(1)}, u32[]{:S(2)}, u32[]{:S(2)}) collective-permute-start(bf16[1,528,256]{2,1,0:T(8,128)(2,1)S(1)} %collective-permute-done.3.refs_3_.refs_0_), channel_id=1, source_target_pairs={{0,2},{2,0},{4,6},{6,4},{8,10},{10,8},{12,14},{14,12},{16,18},{18,... | collective-permute-start | bytes 811016 | tf_op jit(solution)/shard_map/ppermute | solution.py:433
  17.2 3.7 %collective-permute-start.10 = (bf16[1,528,256]{2,1,0:T(8,128)(2,1)S(1)}, bf16[1,528,256]{2,1,0:T(8,128)(2,1)S(1)}, u32[]{:S(2)}, u32[]{:S(2)}) collective-permute-start(bf16[1,528,256]{2,1,0:T(8,128)(2,1)S(1)} %collective-permute-done.2.refs_5_.refs_2_), channel_id=1, source_target_pairs={{0,2},{2,0},{4,6},{6,4},{8,10},{10,8},{12,14},{14,12},{16,18},{18,... | collective-permute-start | bytes 811016 | tf_op jit(solution)/shard_map/ppermute | solution.py:433
  17.7 8.3 %collective-permute-start.7 = (bf16[1,272,256]{2,1,0:T(8,128)(2,1)S(1)}, bf16[1,272,256]{2,1,0:T(8,128)(2,1)S(1)}, u32[]{:S(2)}, u32[]{:S(2)}) collective-permute-start(bf16[1,272,256]{2,1,0:T(8,128)(2,1)S(1)} %bitcast.11), channel_id=1, source_target_pairs={{0,32},{2,34},{4,36},{6,38},{8,40},{10,42},{12,44},{14,46},{16,48}... | collective-permute-start | bytes 417800 | tf_op jit(solution)/shard_map/ppermute | solution.py:445
  21.7 4.3 %copy-start = (bf16[8,528,256]{2,1,0:T(8,128)(2,1)}, bf16[8,528,256]{2,1,0:T(8,128)(2,1)S(1)}, u32[]{:S(2)}) copy-start(bf16[8,528,256]{2,1,0:T(8,128)(2,1)S(1)} %get-tuple-element.43.refs_0_) | copy-start | bytes 6488068
  26.1 6.0 %collective-permute-start.12 = (bf16[2,528,256]{2,1,0:T(8,128)(2,1)S(1)}, bf16[2,528,256]{2,1,0:T(8,128)(2,1)}, u32[]{:S(2)}, u32[]{:S(2)}) collective-permute-start(bf16[2,528,256]{2,1,0:T(8,128)(2,1)S(1)} %collective-permute-done.6.refs_1_.refs_3_.refs_0_), channel_id=1, source_target_pairs={{0,2},{2,0},{4,6},{6,4},{8,10},{10,8},{12,14},{14,12},{16,18},{18,... | collective-permute-start | bytes 1622024 | tf_op jit(solution)/shard_map/ppermute | solution.py:433
  26.2 1.6 %copy-start.1 = (bf16[8,528,256]{2,1,0:T(8,128)(2,1)S(1)}, bf16[8,528,256]{2,1,0:T(8,128)(2,1)}, u32[]{:S(2)}) copy-start(bf16[8,528,256]{2,1,0:T(8,128)(2,1)} %copy-done) | copy-start | bytes 6488068
  26.2 10.6 %collective-permute-start.11 = (bf16[2,528,256]{2,1,0:T(8,128)(2,1)S(1)}, bf16[2,528,256]{2,1,0:T(8,128)(2,1)S(1)}, u32[]{:S(2)}, u32[]{:S(2)}) collective-permute-start(bf16[2,528,256]{2,1,0:T(8,128)(2,1)S(1)} %choose.1), channel_id=1, source_target_pairs={{0,4},{2,14},{4,8},{6,2},{8,12},{10,6},{12,0},{14,10},{16,20},{18,... | collective-permute-start | bytes 1622024 | tf_op jit(solution)/shard_map/ppermute | solution.py:453
  36.9 1.9 %collective-permute-start.13 = (bf16[2,528,256]{2,1,0:T(8,128)(2,1)S(1)}, bf16[2,528,256]{2,1,0:T(8,128)(2,1)S(1)}, u32[]{:S(2)}, u32[]{:S(2)}) collective-permute-start(bf16[2,528,256]{2,1,0:T(8,128)(2,1)S(1)} %collective-permute-done.11.refs_0_), channel_id=1, source_target_pairs={{0,2},{2,0},{4,6},{6,4},{8,10},{10,8},{12,14},{14,12},{16,18},{18,... | collective-permute-start | bytes 1622024 | tf_op jit(solution)/shard_map/ppermute | solution.py:433
  40.6 8.8 %collective-permute-start.14 = (s16[1,272,256]{2,1,0:T(8,128)(2,1)S(1)}, s16[1,272,256]{2,1,0:T(8,128)(2,1)S(1)}, u32[]{:S(2)}, u32[]{:S(2)}) collective-permute-start(s16[1,272,256]{2,1,0:T(8,128)(2,1)S(1)} %attend.11), channel_id=1, source_target_pairs={{32,0},{34,2},{36,4},{38,6},{40,8},{42,10},{44,12},{46,14},{48,16}... | collective-permute-start | bytes 417800 | tf_op jit(solution)/shard_map/ppermute | solution.py:467
  46.1 6.7 %collective-permute-start.16 = (s16[1,272,256]{2,1,0:T(8,128)(2,1)S(1)}, s16[1,272,256]{2,1,0:T(8,128)(2,1)S(1)}, u32[]{:S(2)}, u32[]{:S(2)}) collective-permute-start(s16[1,272,256]{2,1,0:T(8,128)(2,1)S(1)} %get-tuple-element.64), channel_id=1, source_target_pairs={{48,0},{50,2},{52,4},{54,6},{56,8},{58,10},{60,12},{62,14},{0,16},... | collective-permute-start | bytes 417800 | tf_op jit(solution)/shard_map/ppermute | solution.py:470
  46.9 5.8 %copy-start.2 = (s32[256]{0:T(256)S(1)}, s32[256]{0:T(256)}, u32[]{:S(2)}) copy-start(s32[256]{0:T(256)} %param.13) | copy-start | bytes 3076
  46.9 5.8 %collective-permute-start.15 = (s16[1,272,256]{2,1,0:T(8,128)(2,1)S(1)}, s16[1,272,256]{2,1,0:T(8,128)(2,1)S(1)}, u32[]{:S(2)}, u32[]{:S(2)}) collective-permute-start(s16[1,272,256]{2,1,0:T(8,128)(2,1)S(1)} %get-tuple-element.61), channel_id=1, source_target_pairs={{16,0},{18,2},{20,4},{22,6},{24,8},{26,10},{28,12},{30,14},{32,16}... | collective-permute-start | bytes 417800 | tf_op jit(solution)/shard_map/ppermute | solution.py:469

commit v3 on v2

--- a/solution.py
+++ b/solution.py
@@ -376,10 +376,12 @@
     result = jnp.zeros((WIDTH, ROWS), F32)
     tan_result = jnp.zeros((WIDTH, ROWS), F32)
     for weight, (part, _, _, tilt, size, tan_size) in zip(weights, found):
-        mean = part[0:WIDTH, :].astype(jnp.int32).astype(F32) * (size * (1.0 / FULL))
-        tan_mean = part[WIDTH : 2 * WIDTH, :].astype(jnp.int32).astype(F32) * (tan_size * (1.0 / FULL))
-        result += weight * mean
-        tan_result += weight * tan_mean + (weight * (tilt - mean_tilt)) * mean
+        mean = part[0:WIDTH, :].astype(jnp.int32).astype(F32)
+        tan_mean = part[WIDTH : 2 * WIDTH, :].astype(jnp.int32).astype(F32)
+        factor = weight * (size * (1.0 / FULL))
+        tan_factor = weight * (tan_size * (1.0 / FULL))
+        result += factor * mean
+        tan_result += tan_factor * tan_mean + (factor * (tilt - mean_tilt)) * mean
     valid = ids_ref[...] < 2
     out_ref[...] = jnp.where(valid, result, 0.0).T
     tan_ref[...] = jnp.where(valid, tan_result, 0.0).T

time: 54.4 us -> 54.3 us (level)
  Pallas kernels: 19.8 us -> 24.4 us
  waiting for transfers between devices: 11.5 us -> 7.66 us
  starting transfers between devices: 20.2 us -> 19.5 us
    pallas_call x7, Pallas kernels: 14.9 us -> 19.5 us  [attend(): pl.pallas_call(kernel, out_shape=out_shape, in_specs=[VMEM] * len(operand...]
    ppermute x1, waiting for transfers between devices: 2.99 us -> 0.71 us  [per_device(): move(choose(core, (right, level_near), (left, level_near)), perm=BOTH_WAYS)]
    ppermute x6, waiting for transfers between devices: 3.14 us -> 1.55 us  [sibling(): return move(group, perm=SIBLING)]
    ppermute x1, starting transfers between devices: 2.58 us -> 1.84 us  [per_device(): back_far = move(out_far, perm=back(Q_FAR))]
  transfers between devices with their start and end apart: 17 -> 17, of which waited for: 6 -> 5; matrix products, arithmetic and copies ran while one was open for 0% -> 0% of each run, Pallas kernels for 29% -> 38%
where the time goes in v3:
time: 54.3 us; the launch traced here: 53.7 us
  Pallas kernels  24.4 us (45%)
  starting transfers between devices  19.5 us (36%)
  waiting for transfers between devices  7.66 us (14%)
  local copies, waits for them, and re-layouts  1.38 us (3%)
  between operations  0.85 us (2%)
    pallas_call x7, Pallas kernels, attend(): pl.pallas_call(kernel, out_shape=out_shape, in_specs=[VMEM] * len(operand...  19.5 us
    ppermute x2, waiting for transfers between devices, per_device(): q_next, q_last = (move(q, perm=Q_NEXT), move(q, perm=Q_LAST))  3.39 us
    ppermute x2, starting transfers between devices, per_device(): right, left = (move(kv, perm=RIGHT), move(kv, perm=LEFT))  3.24 us
    ppermute x2, starting transfers between devices, per_device(): q_next, q_last = (move(q, perm=Q_NEXT), move(q, perm=Q_LAST))  3.24 us
    ppermute x1, starting transfers between devices, per_device(): q_far = move(q, perm=Q_FAR)  3.19 us
    pallas_call x3, Pallas kernels, gather(): pl.pallas_call(gather_kernel, out_shape=(jax.ShapeDtypeStruct((blocks, KV...  2.54 us
    ppermute x1, starting transfers between devices, per_device(): back_next = move(out_next, perm=back(Q_NEXT))  2.41 us
    ppermute x6, starting transfers between devices, sibling(): return move(group, perm=SIBLING)  2.04 us
  transfers between devices with their start and end apart: 17, of which 5 were waited for; matrix products, arithmetic and copies ran while one was open for 0% of the time, Pallas kernels for 38%

profile of v3, /device:TPU:64, one launch (start us, length us, event | category | flops | bytes accessed | tf_op | source)
XLA Modules:
  0.0 53.7 jit_solution(5667972060280309855)
XLA Ops:
  0.6 1.3 %pack.1 = (bf16[528,256]{1,0:T(8,128)(2,1)S(1)}, bf16[272,256]{1,0:T(8,128)(2,1)S(1)}) custom-call(bf16[256,128]{1,0:T(8,128)(2,1)} %refs_0_.1, bf16[256,128]{1,0:T(8,128)(2,1)} %refs_1_.1, bf16[256,128]{1,0:T(8,128)(2,1)} %refs_2_.1, bf16[256,128]{1,0:T(8,128)(2,1)} %refs_3_.1, bf16[256,128]{1,0:T(8,128)(2,1)} %refs_4_.1, bf16[256,128]{1,0:T(8,128)(2,1)} %refs_5_.1, ...), custom_call_target="tpu_custom_call" | custom-call | flops 1 | bytes 2097152 | tf_op jit(solution)/shard_map/pack/pallas_call | solution.py:64
  1.9 1.7 %collective-permute-start.4 = (bf16[1,528,256]{2,1,0:T(8,128)(2,1)S(1)}, bf16[1,528,256]{2,1,0:T(8,128)(2,1)S(1)}, u32[]{:S(2)}, u32[]{:S(2)}) collective-permute-start(bf16[1,528,256]{2,1,0:T(8,128)(2,1)S(1)} %bitcast.4), channel_id=1, source_target_pairs={{0,64},{2,66},{4,68},{6,70},{8,72},{10,74},{12,76},{14,78},{16,80}... | collective-permute-start | bytes 811016 | tf_op jit(solution)/shard_map/ppermute | solution.py:443
  3.6 1.5 %collective-permute-start.3 = (bf16[1,528,256]{2,1,0:T(8,128)(2,1)S(1)}, bf16[1,528,256]{2,1,0:T(8,128)(2,1)S(1)}, u32[]{:S(2)}, u32[]{:S(2)}) collective-permute-start(bf16[1,528,256]{2,1,0:T(8,128)(2,1)S(1)} %bitcast.5), channel_id=1, source_target_pairs={{0,4},{2,6},{4,8},{6,10},{8,12},{10,14},{12,0},{14,2},{16,20},{18,... | collective-permute-start | bytes 811016 | tf_op jit(solution)/shard_map/ppermute | solution.py:444
  5.1 1.7 %collective-permute-start.2 = (bf16[1,528,256]{2,1,0:T(8,128)(2,1)S(1)}, bf16[1,528,256]{2,1,0:T(8,128)(2,1)S(1)}, u32[]{:S(2)}, u32[]{:S(2)}) collective-permute-start(bf16[1,528,256]{2,1,0:T(8,128)(2,1)S(1)} %bitcast.6), channel_id=1, source_target_pairs={{0,12},{2,14},{4,0},{6,2},{8,4},{10,6},{12,8},{14,10},{16,28},{18,... | collective-permute-start | bytes 811016 | tf_op jit(solution)/shard_map/ppermute | solution.py:444
  6.8 1.6 %collective-permute-start.1 = (bf16[1,272,256]{2,1,0:T(8,128)(2,1)S(1)}, bf16[1,272,256]{2,1,0:T(8,128)(2,1)S(1)}, u32[]{:S(2)}, u32[]{:S(2)}) collective-permute-start(bf16[1,272,256]{2,1,0:T(8,128)(2,1)S(1)} %bitcast.9), channel_id=1, source_target_pairs={{0,16},{2,18},{4,20},{6,22},{8,24},{10,26},{12,28},{14,30},{16,32}... | collective-permute-start | bytes 417800 | tf_op jit(solution)/shard_map/ppermute | solution.py:445
  8.4 1.7 %collective-permute-start = (bf16[1,272,256]{2,1,0:T(8,128)(2,1)S(1)}, bf16[1,272,256]{2,1,0:T(8,128)(2,1)S(1)}, u32[]{:S(2)}, u32[]{:S(2)}) collective-permute-start(bf16[1,272,256]{2,1,0:T(8,128)(2,1)S(1)} %bitcast.10), channel_id=1, source_target_pairs={{0,48},{2,50},{4,52},{6,54},{8,56},{10,58},{12,60},{14,62},{16,0},... | collective-permute-start | bytes 417800 | tf_op jit(solution)/shard_map/ppermute | solution.py:445
  10.1 3.0 %collective-permute-done.1.refs_1_ = bf16[1,272,256]{2,1,0:T(8,128)(2,1)S(1)} collective-permute-done((bf16[1,272,256]{2,1,0:T(8,128)(2,1)S(1)}, bf16[1,272,256]{2,1,0:T(8,128)(2,1)S(1)}, u32[]{:S(2)}, u32[]{:S(2)}) %collective-permute-start.1) | collective-permute-done | bytes 139296 | tf_op jit(solution)/shard_map/ppermute | solution.py:445
  13.1 0.4 collective-permute-done.refs_0_
  13.5 0.0 collective-permute-done.4.refs_0_
  13.5 0.0 collective-permute-done.3.refs_3_.refs_0_
  13.5 0.0 collective-permute-done.2.refs_5_.refs_2_
  13.5 0.1 collective-permute-start.5
  13.6 1.5 %collective-permute-done.5.refs_1_ = bf16[1,528,256]{2,1,0:T(8,128)(2,1)S(1)} collective-permute-done((bf16[1,528,256]{2,1,0:T(8,128)(2,1)S(1)}, bf16[1,528,256]{2,1,0:T(8,128)(2,1)S(1)}, u32[]{:S(2)}, u32[]{:S(2)}) %collective-permute-start.5) | collective-permute-done | bytes 270368 | tf_op jit(solution)/shard_map/ppermute | solution.py:435
  15.1 0.8 %collective-permute-start.6 = (bf16[2,528,256]{2,1,0:T(8,128)(2,1)S(1)}, bf16[2,528,256]{2,1,0:T(8,128)(2,1)S(1)}, u32[]{:S(2)}, u32[]{:S(2)}) collective-permute-start(bf16[2,528,256]{2,1,0:T(8,128)(2,1)S(1)} %stack.3.refs_2_), channel_id=1, source_target_pairs={{0,4},{2,14},{4,8},{6,2},{8,12},{10,6},{12,0},{14,10},{16,20},{18,... | collective-permute-start | bytes 1622024 | tf_op jit(solution)/shard_map/ppermute | solution.py:449
  15.9 1.3 %collective-permute-start.8 = (bf16[1,528,256]{2,1,0:T(8,128)(2,1)S(1)}, bf16[1,528,256]{2,1,0:T(8,128)(2,1)S(1)}, u32[]{:S(2)}, u32[]{:S(2)}) collective-permute-start(bf16[1,528,256]{2,1,0:T(8,128)(2,1)S(1)} %bitcast.7), channel_id=1, source_target_pairs={{0,2},{2,0},{4,6},{6,4},{8,10},{10,8},{12,14},{14,12},{16,18},{18,... | collective-permute-start | bytes 811016 | tf_op jit(solution)/shard_map/ppermute | solution.py:435
  17.2 0.0 collective-permute-start.9
  17.2 0.5 collective-permute-start.10
  17.7 3.2 %collective-permute-start.7 = (bf16[1,272,256]{2,1,0:T(8,128)(2,1)S(1)}, bf16[1,272,256]{2,1,0:T(8,128)(2,1)S(1)}, u32[]{:S(2)}, u32[]{:S(2)}) collective-permute-start(bf16[1,272,256]{2,1,0:T(8,128)(2,1)S(1)} %bitcast.11), channel_id=1, source_target_pairs={{0,32},{2,34},{4,36},{6,38},{8,40},{10,42},{12,44},{14,46},{16,48}... | collective-permute-start | bytes 417800 | tf_op jit(solution)/shard_map/ppermute | solution.py:447
  20.9 0.0 collective-permute-done.8.refs_1_
  21.0 0.0 collective-permute-done.9.refs_4_
  21.0 0.0 collective-permute-done.10.refs_6_
  21.0 0.7 %gather.3 = (bf16[8,528,256]{2,1,0:T(8,128)(2,1)S(1)}, bf16[2048,256]{1,0:T(8,128)(2,1)S(1)}) custom-call(bf16[1,528,256]{2,1,0:T(8,128)(2,1)S(1)} %bitcast.8, bf16[1,528,256]{2,1,0:T(8,128)(2,1)S(1)} %collective-permute-done.8.refs_1_, bf16[2,528,256]{2,1,0:T(8,128)(2,1)S(1)} %stack.3.refs_2_, ...), custom_call_target="tpu_custom_call" | custom-call | flops 1 | bytes 2097152 | tf_op jit(solution)/shard_map/gather/pallas_call | solution.py:183
  21.7 0.0 copy-start
  21.7 4.3 %attend.7.refs_2_ = f32[2,424,256]{2,1,0:T(8,128)S(1)} custom-call(bf16[2,272,256]{2,1,0:T(8,128)(2,1)S(1)} %stack.4.queries, bf16[8,528,256]{2,1,0:T(8,128)(2,1)S(1)} %get-tuple-element.43.refs_0_, bf16[2048,256]{1,0:T(8,128)(2,1)S(1)} %get-tuple-element.44.refs_1_), custom_call_target="tpu_custom_call" | custom-call | flops 1 | bytes 2097152 | tf_op jit(solution)/shard_map/attend/pallas_call | solution.py:348
  26.0 0.0 copy-done
  26.1 0.0 collective-permute-done.7.refs_0_
  26.1 0.0 collective-permute-done.6.refs_1_.refs_3_.refs_0_
  26.1 0.1 collective-permute-start.12
  26.2 0.0 copy-start.1
  26.2 0.2 collective-permute-start.11
  26.4 1.4 %copy-done.1 = bf16[8,528,256]{2,1,0:T(8,128)(2,1)S(1)} copy-done((bf16[8,528,256]{2,1,0:T(8,128)(2,1)S(1)}, bf16[8,528,256]{2,1,0:T(8,128)(2,1)}, u32[]{:S(2)}) %copy-start.1) | copy-done | bytes 2162712
  27.8 4.3 %attend.8.refs_2_ = f32[2,424,256]{2,1,0:T(8,128)S(1)} custom-call(bf16[2,272,256]{2,1,0:T(8,128)(2,1)S(1)} %stack.5.queries, bf16[8,528,256]{2,1,0:T(8,128)(2,1)S(1)} %copy-done.1, bf16[2048,256]{1,0:T(8,128)(2,1)S(1)} %get-tuple-element.44.refs_1_), custom_call_target="tpu_custom_call" | custom-call | flops 2000000000 | bytes 2097152 | tf_op jit(solution)/shard_map/attend/pallas_call | solution.py:348
  32.1 0.0 collective-permute-done.12.refs_1_
  32.1 1.4 %gather.4 = (bf16[4,528,256]{2,1,0:T(8,128)(2,1)S(1)}, bf16[1024,256]{1,0:T(8,128)(2,1)S(1)}) custom-call(bf16[2,528,256]{2,1,0:T(8,128)(2,1)S(1)} %collective-permute-done.6.refs_1_.refs_3_.refs_0_, bf16[2,528,256]{2,1,0:T(8,128)(2,1)} %collective-permute-done.12.refs_1_), custom_call_target="tpu_custom_call" | custom-call | flops 1 | bytes 2097152 | tf_op jit(solution)/shard_map/gather/pallas_call | solution.py:183
  33.5 2.6 %attend.9.refs_2_ = f32[2,424,256]{2,1,0:T(8,128)S(1)} custom-call(bf16[2,272,256]{2,1,0:T(8,128)(2,1)S(1)} %stack.4.queries, bf16[4,528,256]{2,1,0:T(8,128)(2,1)S(1)} %get-tuple-element.49.refs_0_, bf16[1024,256]{1,0:T(8,128)(2,1)S(1)} %get-tuple-element.50.refs_1_, f32[2,424,256]{2,1,0:T(8,128)S(1)} %attend.7.refs_2_), custom_call_target="tpu_custom_call" | custom-call | flops 1 | bytes 2097152 | tf_op jit(solution)/shard_map/attend/pallas_call | solution.py:348
  36.2 0.7 %collective-permute-done.11.refs_0_ = bf16[2,528,256]{2,1,0:T(8,128)(2,1)S(1)} collective-permute-done((bf16[2,528,256]{2,1,0:T(8,128)(2,1)S(1)}, bf16[2,528,256]{2,1,0:T(8,128)(2,1)S(1)}, u32[]{:S(2)}, u32[]{:S(2)}) %collective-permute-start.11) | collective-permute-done | bytes 540704 | tf_op jit(solution)/shard_map/ppermute | solution.py:455
  36.9 0.0 collective-permute-start.13
  36.9 2.6 %attend.10.refs_2_ = f32[2,424,256]{2,1,0:T(8,128)S(1)} custom-call(bf16[2,272,256]{2,1,0:T(8,128)(2,1)S(1)} %stack.5.queries, bf16[4,528,256]{2,1,0:T(8,128)(2,1)S(1)} %get-tuple-element.49.refs_0_, bf16[1024,256]{1,0:T(8,128)(2,1)S(1)} %get-tuple-element.50.refs_1_, f32[2,424,256]{2,1,0:T(8,128)S(1)} %attend.8.refs_2_), custom_call_target="tpu_custom_call" | custom-call | flops 2000000000 | bytes 2097152 | tf_op jit(solution)/shard_map/attend/pallas_call | solution.py:348
  39.5 0.0 collective-permute-done.13.refs_1_
  39.5 0.4 gather.5
  39.9 1.4 %attend.11 = s16[1,272,256]{2,1,0:T(8,128)(2,1)S(1)} custom-call(bf16[2,272,256]{2,1,0:T(8,128)(2,1)S(1)} %stack.5.queries, bf16[4,528,256]{2,1,0:T(8,128)(2,1)S(1)} %get-tuple-element.56.refs_0_, bf16[1024,256]{1,0:T(8,128)(2,1)S(1)} %get-tuple-element.57.refs_1_, f32[2,424,256]{2,1,0:T(8,128)S(1)} %attend.10.refs_2_), custom_call_target="tpu_custom_call" | custom-call | flops 1 | bytes 2097152 | tf_op jit(solution)/shard_map/attend/pallas_call | solution.py:348
  41.4 1.8 %collective-permute-start.14 = (s16[1,272,256]{2,1,0:T(8,128)(2,1)S(1)}, s16[1,272,256]{2,1,0:T(8,128)(2,1)S(1)}, u32[]{:S(2)}, u32[]{:S(2)}) collective-permute-start(s16[1,272,256]{2,1,0:T(8,128)(2,1)S(1)} %attend.11), channel_id=1, source_target_pairs={{32,0},{34,2},{36,4},{38,6},{40,8},{42,10},{44,12},{46,14},{48,16}... | collective-permute-start | bytes 417800 | tf_op jit(solution)/shard_map/ppermute | solution.py:469
  43.2 2.8 %attend.12 = (s16[1,272,256]{2,1,0:T(8,128)(2,1)S(1)}, s16[1,272,256]{2,1,0:T(8,128)(2,1)S(1)}) custom-call(bf16[2,272,256]{2,1,0:T(8,128)(2,1)S(1)} %stack.4.queries, bf16[4,528,256]{2,1,0:T(8,128)(2,1)S(1)} %get-tuple-element.56.refs_0_, bf16[1024,256]{1,0:T(8,128)(2,1)S(1)} %get-tuple-element.57.refs_1_, f32[2,424,256]{2,1,0:T(8,128)S(1)} %attend.9.refs_2_), custom_call_target="tpu_custom_call" | custom-call | flops 1 | bytes 2097152 | tf_op jit(solution)/shard_map/attend/pallas_call | solution.py:348
  46.1 0.9 %collective-permute-start.16 = (s16[1,272,256]{2,1,0:T(8,128)(2,1)S(1)}, s16[1,272,256]{2,1,0:T(8,128)(2,1)S(1)}, u32[]{:S(2)}, u32[]{:S(2)}) collective-permute-start(s16[1,272,256]{2,1,0:T(8,128)(2,1)S(1)} %get-tuple-element.64), channel_id=1, source_target_pairs={{48,0},{50,2},{52,4},{54,6},{56,8},{58,10},{60,12},{62,14},{0,16},... | collective-permute-start | bytes 417800 | tf_op jit(solution)/shard_map/ppermute | solution.py:472
  46.9 0.0 copy-start.2
  46.9 2.4 %collective-permute-start.15 = (s16[1,272,256]{2,1,0:T(8,128)(2,1)S(1)}, s16[1,272,256]{2,1,0:T(8,128)(2,1)S(1)}, u32[]{:S(2)}, u32[]{:S(2)}) collective-permute-start(s16[1,272,256]{2,1,0:T(8,128)(2,1)S(1)} %get-tuple-element.61), channel_id=1, source_target_pairs={{16,0},{18,2},{20,4},{22,6},{24,8},{26,10},{28,12},{30,14},{32,16}... | collective-permute-start | bytes 417800 | tf_op jit(solution)/shard_map/ppermute | solution.py:471
  49.4 0.0 collective-permute-done.14.refs_3_
  49.4 1.4 %attend.13.refs_0_ = s16[1,272,256]{2,1,0:T(8,128)(2,1)S(1)} custom-call(bf16[2,272,256]{2,1,0:T(8,128)(2,1)S(1)} %stack.5.queries, bf16[4,528,256]{2,1,0:T(8,128)(2,1)S(1)} %get-tuple-element.56.refs_0_, bf16[1024,256]{1,0:T(8,128)(2,1)S(1)} %get-tuple-element.57.refs_1_, f32[2,424,256]{2,1,0:T(8,128)S(1)} %attend.10.refs_2_), custom_call_target="tpu_custom_call" | custom-call | flops 1 | bytes 2097152 | tf_op jit(solution)/shard_map/attend/pallas_call | solution.py:348
  50.8 2.0 %collective-permute-done.16.refs_2_ = s16[1,272,256]{2,1,0:T(8,128)(2,1)S(1)} collective-permute-done((s16[1,272,256]{2,1,0:T(8,128)(2,1)S(1)}, s16[1,272,256]{2,1,0:T(8,128)(2,1)S(1)}, u32[]{:S(2)}, u32[]{:S(2)}) %collective-permute-start.16) | collective-permute-done | bytes 139296 | tf_op jit(solution)/shard_map/ppermute | solution.py:472
  52.8 0.0 collective-permute-done.15.refs_1_
  52.8 0.0 copy-done.2
  52.8 0.9 %combine.1 = (f32[256,128]{1,0:T(8,128)}, f32[256,128]{1,0:T(8,128)}) custom-call(s32[1,256]{1,0:T(1,128)S(1)} %bitcast.14, s16[1,272,256]{2,1,0:T(8,128)(2,1)S(1)} %attend.13.refs_0_, s16[1,272,256]{2,1,0:T(8,128)(2,1)S(1)} %collective-permute-done.15.refs_1_, s16[1,272,256]{2,1,0:T(8,128)(2,1)S(1)} %collective-permute-done.16.refs_2_, ...), custom_call_target="tpu_custom_call" | custom-call | flops 1 | bytes 2097152 | tf_op jit(solution)/shard_map/combine/pallas_call | solution.py:392
  (4 shorter events, 0.1 us)
Async XLA Ops:
  1.9 11.6 %collective-permute-start.4 = (bf16[1,528,256]{2,1,0:T(8,128)(2,1)S(1)}, bf16[1,528,256]{2,1,0:T(8,128)(2,1)S(1)}, u32[]{:S(2)}, u32[]{:S(2)}) collective-permute-start(bf16[1,528,256]{2,1,0:T(8,128)(2,1)S(1)} %bitcast.4), channel_id=1, source_target_pairs={{0,64},{2,66},{4,68},{6,70},{8,72},{10,74},{12,76},{14,78},{16,80}... | collective-permute-start | bytes 811016 | tf_op jit(solution)/shard_map/ppermute | solution.py:443
  3.6 9.9 %collective-permute-start.3 = (bf16[1,528,256]{2,1,0:T(8,128)(2,1)S(1)}, bf16[1,528,256]{2,1,0:T(8,128)(2,1)S(1)}, u32[]{:S(2)}, u32[]{:S(2)}) collective-permute-start(bf16[1,528,256]{2,1,0:T(8,128)(2,1)S(1)} %bitcast.5), channel_id=1, source_target_pairs={{0,4},{2,6},{4,8},{6,10},{8,12},{10,14},{12,0},{14,2},{16,20},{18,... | collective-permute-start | bytes 811016 | tf_op jit(solution)/shard_map/ppermute | solution.py:444
  5.1 8.4 %collective-permute-start.2 = (bf16[1,528,256]{2,1,0:T(8,128)(2,1)S(1)}, bf16[1,528,256]{2,1,0:T(8,128)(2,1)S(1)}, u32[]{:S(2)}, u32[]{:S(2)}) collective-permute-start(bf16[1,528,256]{2,1,0:T(8,128)(2,1)S(1)} %bitcast.6), channel_id=1, source_target_pairs={{0,12},{2,14},{4,0},{6,2},{8,4},{10,6},{12,8},{14,10},{16,28},{18,... | collective-permute-start | bytes 811016 | tf_op jit(solution)/shard_map/ppermute | solution.py:444
  6.8 6.3 %collective-permute-start.1 = (bf16[1,272,256]{2,1,0:T(8,128)(2,1)S(1)}, bf16[1,272,256]{2,1,0:T(8,128)(2,1)S(1)}, u32[]{:S(2)}, u32[]{:S(2)}) collective-permute-start(bf16[1,272,256]{2,1,0:T(8,128)(2,1)S(1)} %bitcast.9), channel_id=1, source_target_pairs={{0,16},{2,18},{4,20},{6,22},{8,24},{10,26},{12,28},{14,30},{16,32}... | collective-permute-start | bytes 417800 | tf_op jit(solution)/shard_map/ppermute | solution.py:445
  8.4 5.1 %collective-permute-start = (bf16[1,272,256]{2,1,0:T(8,128)(2,1)S(1)}, bf16[1,272,256]{2,1,0:T(8,128)(2,1)S(1)}, u32[]{:S(2)}, u32[]{:S(2)}) collective-permute-start(bf16[1,272,256]{2,1,0:T(8,128)(2,1)S(1)} %bitcast.10), channel_id=1, source_target_pairs={{0,48},{2,50},{4,52},{6,54},{8,56},{10,58},{12,60},{14,62},{16,0},... | collective-permute-start | bytes 417800 | tf_op jit(solution)/shard_map/ppermute | solution.py:445
  13.5 1.6 %collective-permute-start.5 = (bf16[1,528,256]{2,1,0:T(8,128)(2,1)S(1)}, bf16[1,528,256]{2,1,0:T(8,128)(2,1)S(1)}, u32[]{:S(2)}, u32[]{:S(2)}) collective-permute-start(bf16[1,528,256]{2,1,0:T(8,128)(2,1)S(1)} %collective-permute-done.4.refs_0_), channel_id=1, source_target_pairs={{0,2},{2,0},{4,6},{6,4},{8,10},{10,8},{12,14},{14,12},{16,18},{18,... | collective-permute-start | bytes 811016 | tf_op jit(solution)/shard_map/ppermute | solution.py:435
  15.1 10.9 %collective-permute-start.6 = (bf16[2,528,256]{2,1,0:T(8,128)(2,1)S(1)}, bf16[2,528,256]{2,1,0:T(8,128)(2,1)S(1)}, u32[]{:S(2)}, u32[]{:S(2)}) collective-permute-start(bf16[2,528,256]{2,1,0:T(8,128)(2,1)S(1)} %stack.3.refs_2_), channel_id=1, source_target_pairs={{0,4},{2,14},{4,8},{6,2},{8,12},{10,6},{12,0},{14,10},{16,20},{18,... | collective-permute-start | bytes 1622024 | tf_op jit(solution)/shard_map/ppermute | solution.py:449
  15.9 5.1 %collective-permute-start.8 = (bf16[1,528,256]{2,1,0:T(8,128)(2,1)S(1)}, bf16[1,528,256]{2,1,0:T(8,128)(2,1)S(1)}, u32[]{:S(2)}, u32[]{:S(2)}) collective-permute-start(bf16[1,528,256]{2,1,0:T(8,128)(2,1)S(1)} %bitcast.7), channel_id=1, source_target_pairs={{0,2},{2,0},{4,6},{6,4},{8,10},{10,8},{12,14},{14,12},{16,18},{18,... | collective-permute-start | bytes 811016 | tf_op jit(solution)/shard_map/ppermute | solution.py:435
  17.2 3.7 %collective-permute-start.9 = (bf16[1,528,256]{2,1,0:T(8,128)(2,1)S(1)}, bf16[1,528,256]{2,1,0:T(8,128)(2,1)S(1)}, u32[]{:S(2)}, u32[]{:S(2)}) collective-permute-start(bf16[1,528,256]{2,1,0:T(8,128)(2,1)S(1)} %collective-permute-done.3.refs_3_.refs_0_), channel_id=1, source_target_pairs={{0,2},{2,0},{4,6},{6,4},{8,10},{10,8},{12,14},{14,12},{16,18},{18,... | collective-permute-start | bytes 811016 | tf_op jit(solution)/shard_map/ppermute | solution.py:435
  17.2 3.7 %collective-permute-start.10 = (bf16[1,528,256]{2,1,0:T(8,128)(2,1)S(1)}, bf16[1,528,256]{2,1,0:T(8,128)(2,1)S(1)}, u32[]{:S(2)}, u32[]{:S(2)}) collective-permute-start(bf16[1,528,256]{2,1,0:T(8,128)(2,1)S(1)} %collective-permute-done.2.refs_5_.refs_2_), channel_id=1, source_target_pairs={{0,2},{2,0},{4,6},{6,4},{8,10},{10,8},{12,14},{14,12},{16,18},{18,... | collective-permute-start | bytes 811016 | tf_op jit(solution)/shard_map/ppermute | solution.py:435
  17.7 8.3 %collective-permute-start.7 = (bf16[1,272,256]{2,1,0:T(8,128)(2,1)S(1)}, bf16[1,272,256]{2,1,0:T(8,128)(2,1)S(1)}, u32[]{:S(2)}, u32[]{:S(2)}) collective-permute-start(bf16[1,272,256]{2,1,0:T(8,128)(2,1)S(1)} %bitcast.11), channel_id=1, source_target_pairs={{0,32},{2,34},{4,36},{6,38},{8,40},{10,42},{12,44},{14,46},{16,48}... | collective-permute-start | bytes 417800 | tf_op jit(solution)/shard_map/ppermute | solution.py:447
  21.7 4.3 %copy-start = (bf16[8,528,256]{2,1,0:T(8,128)(2,1)}, bf16[8,528,256]{2,1,0:T(8,128)(2,1)S(1)}, u32[]{:S(2)}) copy-start(bf16[8,528,256]{2,1,0:T(8,128)(2,1)S(1)} %get-tuple-element.43.refs_0_) | copy-start | bytes 6488068
  26.1 6.0 %collective-permute-start.12 = (bf16[2,528,256]{2,1,0:T(8,128)(2,1)S(1)}, bf16[2,528,256]{2,1,0:T(8,128)(2,1)}, u32[]{:S(2)}, u32[]{:S(2)}) collective-permute-start(bf16[2,528,256]{2,1,0:T(8,128)(2,1)S(1)} %collective-permute-done.6.refs_1_.refs_3_.refs_0_), channel_id=1, source_target_pairs={{0,2},{2,0},{4,6},{6,4},{8,10},{10,8},{12,14},{14,12},{16,18},{18,... | collective-permute-start | bytes 1622024 | tf_op jit(solution)/shard_map/ppermute | solution.py:435
  26.2 1.6 %copy-start.1 = (bf16[8,528,256]{2,1,0:T(8,128)(2,1)S(1)}, bf16[8,528,256]{2,1,0:T(8,128)(2,1)}, u32[]{:S(2)}) copy-start(bf16[8,528,256]{2,1,0:T(8,128)(2,1)} %copy-done) | copy-start | bytes 6488068
  26.2 10.6 %collective-permute-start.11 = (bf16[2,528,256]{2,1,0:T(8,128)(2,1)S(1)}, bf16[2,528,256]{2,1,0:T(8,128)(2,1)S(1)}, u32[]{:S(2)}, u32[]{:S(2)}) collective-permute-start(bf16[2,528,256]{2,1,0:T(8,128)(2,1)S(1)} %choose.1), channel_id=1, source_target_pairs={{0,4},{2,14},{4,8},{6,2},{8,12},{10,6},{12,0},{14,10},{16,20},{18,... | collective-permute-start | bytes 1622024 | tf_op jit(solution)/shard_map/ppermute | solution.py:455
  36.9 2.7 %collective-permute-start.13 = (bf16[2,528,256]{2,1,0:T(8,128)(2,1)S(1)}, bf16[2,528,256]{2,1,0:T(8,128)(2,1)S(1)}, u32[]{:S(2)}, u32[]{:S(2)}) collective-permute-start(bf16[2,528,256]{2,1,0:T(8,128)(2,1)S(1)} %collective-permute-done.11.refs_0_), channel_id=1, source_target_pairs={{0,2},{2,0},{4,6},{6,4},{8,10},{10,8},{12,14},{14,12},{16,18},{18,... | collective-permute-start | bytes 1622024 | tf_op jit(solution)/shard_map/ppermute | solution.py:435
  41.4 8.0 %collective-permute-start.14 = (s16[1,272,256]{2,1,0:T(8,128)(2,1)S(1)}, s16[1,272,256]{2,1,0:T(8,128)(2,1)S(1)}, u32[]{:S(2)}, u32[]{:S(2)}) collective-permute-start(s16[1,272,256]{2,1,0:T(8,128)(2,1)S(1)} %attend.11), channel_id=1, source_target_pairs={{32,0},{34,2},{36,4},{38,6},{40,8},{42,10},{44,12},{46,14},{48,16}... | collective-permute-start | bytes 417800 | tf_op jit(solution)/shard_map/ppermute | solution.py:469
  46.1 6.7 %collective-permute-start.16 = (s16[1,272,256]{2,1,0:T(8,128)(2,1)S(1)}, s16[1,272,256]{2,1,0:T(8,128)(2,1)S(1)}, u32[]{:S(2)}, u32[]{:S(2)}) collective-permute-start(s16[1,272,256]{2,1,0:T(8,128)(2,1)S(1)} %get-tuple-element.64), channel_id=1, source_target_pairs={{48,0},{50,2},{52,4},{54,6},{56,8},{58,10},{60,12},{62,14},{0,16},... | collective-permute-start | bytes 417800 | tf_op jit(solution)/shard_map/ppermute | solution.py:472
  46.9 5.8 %copy-start.2 = (s32[256]{0:T(256)S(1)}, s32[256]{0:T(256)}, u32[]{:S(2)}) copy-start(s32[256]{0:T(256)} %param.13) | copy-start | bytes 3076
  46.9 5.8 %collective-permute-start.15 = (s16[1,272,256]{2,1,0:T(8,128)(2,1)S(1)}, s16[1,272,256]{2,1,0:T(8,128)(2,1)S(1)}, u32[]{:S(2)}, u32[]{:S(2)}) collective-permute-start(s16[1,272,256]{2,1,0:T(8,128)(2,1)S(1)} %get-tuple-element.61), channel_id=1, source_target_pairs={{16,0},{18,2},{20,4},{22,6},{24,8},{26,10},{28,12},{30,14},{32,16}... | collective-permute-start | bytes 417800 | tf_op jit(solution)/shard_map/ppermute | solution.py:471
